TPU v7x, 32 devices: a whole 2x2x4 slice. The times are simulated.
32 devices in a mesh: sect: 2 (over core), cols: 16 (over z, y, x).
Axes of the slice: x: 2, y: 2, z: 4, core: 2. Of those that a mesh axis runs over, the one named last changes fastest.
Arguments:
- air_state: float32 [64, 6, 98304], P('sect', None, 'cols'), may hold values from -6 to 6
- mix_coef: float32 [64, 98304], P('sect', 'cols'), may hold values from 0.1 to 1600
- flux_scale: float32 [98304], P('cols'), may hold values from 0.5 to 4
- sea_state: float32 [6, 98304], P(None, ('sect', 'cols')), may hold values from -6 to 6
- sea_rate: float32 [98304], P(('sect', 'cols')), may hold values from 0.5 to 4
- block_counts: int32 [32, 48], P(('sect', 'cols')), may hold values from 1 to 256, 9830 in all within a row
- cell_column: int32 [393216], P(('sect', 'cols')), may hold values from 0 to 127
- cell_owner: int32 [393216, 1], P(('sect', 'cols')), may hold values from 0 to 31; in each aligned block of 12288 rows (0 to 12287, 12288 to 24575, ...) at most 480 rows name the same one
- cell_coef: float32 [393216], P(('sect', 'cols')), may hold values from 0.3 to 3
- cell_weight: float32 [393216], P(('sect', 'cols')), may hold values from 0.1 to 0.5
- slot_cell: int32 [491520], P(('sect', 'cols')), may hold values from 0 to 3071
- slot_frac: float32 [491520], P(('sect', 'cols')), may hold values from 0.2 to 1
Outputs:
- air_new: float32 [64, 6, 98304], P('sect', None, 'cols')
- sea_new: float32 [6, 98304], P(None, ('sect', 'cols'))
Inputs may be any that keep to these rules, and one draw needn't show every extreme that they name: `cell_owner`: among the slots of one device (aligned blocks of 12288 rows) no surface device is named more than 480 times, and some surface device exactly 480 times. `block_counts`: each device's counts have the same sum, and one block of every device is full.
All inputs are finite; a program needn't handle non-finite values.
Results may differ from a plain program's by a relative error of at most 0.0003.
Values sent between devices are 32-bit elements; how exact they have to be, the bound alone decides.
A program may use at most 128 MiB of HBM per device.

v0:
```python
import jax
import jax.numpy as jnp
from jax import lax
from jax.sharding import PartitionSpec as P

BLOCK_COLS = 128
BLOCK_SLOTS = 256
SUBSTEPS = 2


cell_group = 64


def shifted(value, axis, steps):
    count = lax.axis_size(axis)
    initial, last = (max(0, -steps), min(count, count - steps))
    return lax.ppermute(value, axis, [(source, source + steps) for source in range(initial, last)])


def descend(mix_coef, air_state, under_start, part_start):

    def level_down(carried, inputs):
        under, upper_part = carried
        coupling, column_values = inputs
        denom = 1.0 + coupling + under
        part = (column_values + upper_part) / denom
        ratio = coupling / denom
        return ((coupling * (1.0 - ratio), coupling * part), (part, denom))

    (under_end, part_end), (parts, denoms) = lax.scan(
        level_down, (under_start, part_start), (mix_coef, air_state), unroll=8
    )
    return (parts, denoms, jnp.concatenate([under_end[None], part_end], axis=0))


def ascend(parts, ratios, below_start):

    def level_up(below, inputs):
        part, ratio = inputs
        value = part + ratio * below
        return (value, value)

    _, values = lax.scan(level_up, below_start, (parts, ratios), reverse=True, unroll=8)
    return values


def body(
    air_state,
    mix_coef,
    flux_scale,
    sea_state,
    sea_rate,
    block_counts,
    cell_column,
    cell_owner,
    cell_coef,
    cell_weight,
    slot_cell,
    slot_frac,
):
    levels, tracers, columns = air_state.shape
    is_lower = lax.axis_index("sect") == 1
    sections = lax.axis_size("sect")
    devices = sections * lax.axis_size("cols")
    highest = lax.Precision.HIGHEST

    def upper_sweep():
        return descend(
            mix_coef,
            air_state,
            jnp.zeros((columns,), jnp.float32),
            jnp.zeros((tracers, columns), jnp.float32),
        )

    def empty_sweep():
        return (
            jnp.zeros_like(air_state),
            jnp.zeros_like(mix_coef),
            jnp.zeros((tracers + 1, columns), jnp.float32),
        )

    first_sweep = lax.cond(is_lower, empty_sweep, upper_sweep)
    handed = shifted(first_sweep[2], "sect", 1)

    def lower_sweep():
        return descend(mix_coef, air_state, handed[0], handed[1:])

    def keep_sweep():
        return first_sweep

    parts, denoms, unused_end = lax.cond(is_lower, lower_sweep, keep_sweep)
    ratios = mix_coef / denoms
    resid_share = jnp.where(is_lower, parts[-1], 0.0)
    slope_share = jnp.where(is_lower, flux_scale / denoms[-1], 0.0)
    slot_count = cell_column.shape[0]
    block_total = slot_count // BLOCK_SLOTS
    recv_len = slot_cell.shape[0]
    capacity = recv_len // devices
    surf_cells = sea_state.shape[1]
    groups = surf_cells // cell_group
    in_block = lax.broadcasted_iota(jnp.int32, (block_total, BLOCK_SLOTS), 1)
    live = (in_block < block_counts[0][:, None]).astype(jnp.float32).reshape(slot_count)
    gain = cell_coef * live
    col_weight = cell_weight * gain
    colmap = (
        cell_column.reshape(block_total, BLOCK_SLOTS)[:, :, None]
        == lax.broadcasted_iota(jnp.int32, (block_total, BLOCK_SLOTS, BLOCK_COLS), 2)
    ).astype(jnp.float32)
    owner = cell_owner[:, 0]
    ownermap = (
        owner.reshape(block_total, BLOCK_SLOTS)[:, :, None]
        == lax.broadcasted_iota(jnp.int32, (block_total, BLOCK_SLOTS, devices), 2)
    ).astype(jnp.float32)
    lower_tri = (
        lax.broadcasted_iota(jnp.int32, (BLOCK_SLOTS, BLOCK_SLOTS), 0)
        >= lax.broadcasted_iota(jnp.int32, (BLOCK_SLOTS, BLOCK_SLOTS), 1)
    ).astype(jnp.float32)
    running = jnp.einsum("xy,nyd->nxd", lower_tri, ownermap, precision=highest)
    block_sums = running[:, -1, :]
    offsets = jnp.cumsum(block_sums, axis=0) - block_sums
    order_in = (jnp.sum((running + offsets[:, None, :]) * ownermap, axis=2) - 1.0).reshape(
        slot_count
    )
    owner_flat = ownermap.reshape(slot_count, devices)
    rank_map = (
        order_in[:, None]
        == lax.broadcasted_iota(jnp.int32, (slot_count, capacity), 1).astype(jnp.float32)
    ).astype(jnp.float32)
    group_map = (
        (slot_cell // cell_group)[:, None] == lax.broadcasted_iota(jnp.int32, (recv_len, groups), 1)
    ).astype(jnp.float32)
    member_map = (
        (slot_cell % cell_group)[:, None]
        == lax.broadcasted_iota(jnp.int32, (recv_len, cell_group), 1)
    ).astype(jnp.float32)
    flux_part = jnp.zeros((tracers, columns), jnp.float32)
    sea = sea_state
    bottom = resid_share
    for step in range(SUBSTEPS + 1):
        flux_col, resid, slope = lax.psum((flux_part, resid_share, slope_share), "sect")
        bottom = resid + slope * flux_col
        if step < SUBSTEPS:
            at_cells = jnp.einsum(
                "nxb,tnb->tnx",
                colmap,
                bottom.reshape(tracers, block_total, BLOCK_COLS),
                precision=highest,
            ).reshape(tracers, slot_count)
            payload = jnp.concatenate([at_cells, gain[None]], axis=0)
            spread = payload[:, :, None] * rank_map[None]
            outgoing = jnp.einsum("ed,ter->tdr", owner_flat, spread, precision=highest).reshape(
                tracers + 1, recv_len
            )
            arrived = lax.all_to_all(
                outgoing, ("sect", "cols"), split_axis=1, concat_axis=1, tiled=True
            )
            coupling_slot = arrived[tracers] * slot_frac
            values = jnp.concatenate(
                [coupling_slot[None] * arrived[:tracers], coupling_slot[None]], axis=0
            )
            placed = values[:, :, None] * member_map[None]
            summed = jnp.einsum("sh,tsl->thl", group_map, placed, precision=highest).reshape(
                tracers + 1, surf_cells
            )
            numer = summed[:tracers]
            total = summed[tracers]
            sea = (sea + sea_rate * numer) / (1.0 + sea_rate * total)
            picked = jnp.einsum(
                "sh,thl->tsl",
                group_map,
                sea.reshape(tracers, groups, cell_group),
                precision=highest,
            )
            returning = jnp.sum(picked * member_map[None], axis=2)
            returned = lax.all_to_all(
                returning, ("sect", "cols"), split_axis=1, concat_axis=1, tiled=True
            )
            by_owner = jnp.einsum(
                "ed,tdr->ter",
                owner_flat,
                returned.reshape(tracers, devices, capacity),
                precision=highest,
            )
            seen = jnp.sum(by_owner * rank_map[None], axis=2)
            flux = col_weight * (seen - at_cells)
            flux_part = jnp.einsum(
                "nxb,tnx->tnb",
                colmap,
                flux.reshape(tracers, block_total, BLOCK_SLOTS),
                precision=highest,
            ).reshape(tracers, columns)

    def lower_rise():
        return ascend(parts[:-1], ratios[:-1], bottom)

    def empty_rise():
        return jnp.zeros((levels - 1, tracers, columns), jnp.float32)

    rising = lax.cond(is_lower, lower_rise, empty_rise)
    from_below = shifted(rising[0], "sect", -1)

    def lower_final():
        return jnp.concatenate([rising, bottom[None]], axis=0)

    def upper_final():
        return ascend(parts, ratios, from_below)

    air_new = lax.cond(is_lower, lower_final, upper_final)
    return (air_new, sea)


def solution(mesh):
    return jax.shard_map(
        body,
        mesh=mesh,
        in_specs=(
            P("sect", None, "cols"),
            P("sect", "cols"),
            P("cols"),
            P(None, ("sect", "cols")),
            P(("sect", "cols")),
            P(("sect", "cols"), None),
            P(("sect", "cols")),
            P(("sect", "cols"), None),
            P(("sect", "cols")),
            P(("sect", "cols")),
            P(("sect", "cols")),
            P(("sect", "cols")),
        ),
        out_specs=(P("sect", None, "cols"), P(None, ("sect", "cols"))),
        check_vma=False,
    )
```

profile of v0, /device:TPU:0, one launch (start us, length us, event | category | flops | bytes accessed | tf_op | source)
XLA Modules:
  0.0 741.9 jit_solution(16347808423419156510)
XLA Ops:
  7.2 58.9 %conditional.4 = (f32[32,6,6144]{2,1,0:T(8,128)}, f32[32,6144]{1,0:T(8,128)}, f32[7,6144]{1,0:T(8,128)S(1)}) conditional(s32[]{:T(128)} %convert_element_type.30, (f32[32,6144]{1,0:T(8,128)}, f32[32,6,6144]{2,0,1:T(8,128)}) %tuple.97, () %tuple.98), branch_computations={%region_0.3_spmd, %region_3.4_spmd} | conditional | flops 1658889 | bytes 20668940 | solution.py:82
  7.3 7.8 %copy.96 = f32[32,6,6144]{2,1,0:T(8,128)} copy(f32[32,6,6144]{2,0,1:T(8,128)} %get-tuple-element.429) | data formatting | bytes 9437184 | tf_op jit(solution)/shard_map
  15.1 51.0 %while.63 = (s32[]{:T(128)}, f32[6144]{0:T(1024)S(1)}, f32[6,6144]{1,0:T(8,128)S(1)}, f32[4,8,6,6144]{3,2,1,0:T(8,128)}, f32[4,8,6144]{2,1,0:T(8,128)}, /*index=...) while((s32[]{:T(128)}, f32[6144]{0:T(1024)S(1)}, ...), condition=%wide.region_2.2_spmd.clone, body=%wide.region_1.1_spmd.clone.sunk | while | flops 1615881 | bytes 10887533 | solution.py:30
  15.1 1.9 constant_dynamic-slice_fusion.39
  22.3 1.1 bitcast_dynamic-update-slice_fusion.116
  24.4 1.1 bitcast_dynamic-update-slice_fusion.118
  25.6 1.2 bitcast_dynamic-update-slice_fusion.119
  27.8 2.0 constant_dynamic-slice_fusion.39
  35.1 1.1 bitcast_dynamic-update-slice_fusion.116
  38.3 1.3 bitcast_dynamic-update-slice_fusion.119
  40.6 1.9 constant_dynamic-slice_fusion.39
  47.8 1.1 bitcast_dynamic-update-slice_fusion.116
  51.1 1.3 bitcast_dynamic-update-slice_fusion.119
  53.4 2.0 constant_dynamic-slice_fusion.39
  60.6 1.1 bitcast_dynamic-update-slice_fusion.116
  63.9 1.2 bitcast_dynamic-update-slice_fusion.119
  66.1 1.5 collective-permute-start
  69.7 4.8 copy.100
  74.9 4.5 copy.101
  81.0 3.7 select_reduce_fusion
  85.2 10.7 %compare_convert_fusion = f32[12288,480]{0,1:T(8,128)} fusion(f32[12288]{0:T(1024)S(1)} %bitcast.886, f32[480]{0:T(512)S(1)} %iota_convert_fusion), kind=kLoop, calls=%fused_computation.208 | loop fusion | flops 11796480 | bytes 23644032 | tf_op jit(solution)/shard_map/convert_element_type | solution.py:128
  96.1 1.4 conditional.5
  97.5 1.6 fusion.122
  99.2 34.9 %psum.29 = f32[6144]{0:T(1024)S(1)} all-reduce(f32[6144]{0:T(1024)S(1)} %divide_select_fusion), channel_id=1, replica_groups=mesh['sect'=2,'cols'=16] {'sect'}, use_global_device_ids=true, to_apply=%region_9.10 | all-reduce | flops 6144 | bytes 49152 | tf_op jit(solution)/shard_map/psum | solution.py:140
  134.1 17.3 %all-reduce.4.cloned.1.call-done = f32[6,6144]{1,0:T(8,128)} async-done(((f32[6,6144]{1,0:T(8,128)}), f32[6,6144]{1,0:T(8,128)}) %all-reduce.4.cloned.1.call-update) | async-done | bytes 147472 | tf_op jit(solution)/shard_map/psum | solution.py:140
  151.4 5.9 fusion.69
  157.4 83.3 %fusion.89 = f32[7,32,480]{2,1,0:T(8,128)S(1)} fusion(f32[12288,480]{0,1:T(8,128)} %compare_convert_fusion, f32[7,12288]{1,0:T(8,128)S(1)} %pad_maximum_fusion.3, pred[12288,32,1]{0,1,2:T(32,128)(4,1)S(1)} %fusion.172), kind=kOutput, calls=%fused_computation.234 | convolution fusion | flops 15895756800 | bytes 24760320 | tf_op jit(solution)/shard_map/ed,ter->tdr/dot_general | solution.py:151
  241.8 5.9 all-to-all-start
  247.7 2.2 fusion.70
  250.0 14.6 %all-to-all-done = f32[7,32,480]{2,0,1:T(8,128)S(1)} async-done(((f32[7,32,480]{2,0,1:T(8,128)}), f32[7,32,480]{2,0,1:T(8,128)S(1)}, u32[]{:S(2)}, u32[]{:S(2)}) %all-to-all-start) | async-done | bytes 430112 | tf_op jit(solution)/shard_map/all_to_all | solution.py:154
  265.6 20.5 %fusion.99 = f32[7,48,64]{2,1,0:T(8,128)S(1)} fusion(s32[15360]{0:T(1024)S(1)} %get-tuple-element.577, f32[15360,64]{0,1:T(8,128)} %fusion.70, f32[7,15360]{1,0:T(8,128)S(1)} %pad_maximum_fusion.4), kind=kOutput, calls=%fused_computation.236 | convolution fusion | flops 3971235840 | bytes 4509696 | tf_op jit(solution)/shard_map/sh,tsl->thl/dot_general | solution.py:162
  286.5 12.4 %fusion.63 = f32[6,15360]{1,0:T(8,128)S(1)} fusion(f32[6,48,64]{2,1,0:T(8,128)S(1)} %reshape.369, f32[15360,64]{0,1:T(8,128)} %fusion.70, s32[15360]{0:T(1024)S(1)} %get-tuple-element.577), kind=kOutput, calls=%fused_computation.207 | convolution fusion | flops 3409827840 | bytes 4435968 | tf_op jit(solution)/shard_map/sh,thl->tsl/dot_general | solution.py:168
  300.2 2.6 all-to-all-start.1
  302.9 16.7 %all-to-all-done.1 = f32[6,32,480]{2,0,1:T(8,128)S(1)} async-done(((f32[6,32,480]{2,0,1:T(8,128)}), f32[6,32,480]{2,0,1:T(8,128)S(1)}, u32[]{:S(2)}, u32[]{:S(2)}) %all-to-all-start.1) | async-done | bytes 368672 | tf_op jit(solution)/shard_map/all_to_all | solution.py:175
  319.7 62.2 %fusion.53 = f32[6,12288]{1,0:T(8,128)S(1)} fusion(f32[12288,480]{0,1:T(8,128)} %compare_convert_fusion, s32[12288]{0:T(1024)S(1)} %bitcast.866, f32[6,32,480]{2,0,1:T(8,128)S(1)} %all-to-all-done.1), kind=kOutput, calls=%fused_computation.195 | convolution fusion | flops 13660643328 | bytes 24305664 | tf_op jit(solution)/shard_map/ed,tdr->ter/dot_general | solution.py:178
  381.9 4.9 convolution_bitcast_fusion.1
  387.1 14.7 %all-reduce.6.cloned.1.call-done = f32[6,6144]{1,0:T(8,128)} async-done(((f32[6,6144]{1,0:T(8,128)}), f32[6,6144]{1,0:T(8,128)}) %all-reduce.6.cloned.1.call-update) | async-done | bytes 147472 | tf_op jit(solution)/shard_map/psum | solution.py:140
  401.7 6.4 fusion.68
  408.2 83.3 %fusion.94 = f32[7,32,480]{2,1,0:T(8,128)S(1)} fusion(f32[7,12288]{1,0:T(8,128)S(1)} %pad_maximum_fusion.2, f32[12288,480]{0,1:T(8,128)} %compare_convert_fusion, pred[12288,32,1]{0,1,2:T(32,128)(4,1)S(1)} %fusion.174), kind=kOutput, calls=%fused_computation.235 | convolution fusion | flops 15895756800 | bytes 24760320 | tf_op jit(solution)/shard_map/ed,ter->tdr/dot_general | solution.py:151
  491.8 22.6 %all_to_all.30 = f32[7,32,480]{2,0,1:T(8,128)S(1)} all-to-all(f32[7,32,480]{2,0,1:T(8,128)S(1)} %copy.110), channel_id=1, replica_groups=mesh['sect'=2,'cols'=16] {'sect','cols'}, dimensions={1} | all-to-all | bytes 860160 | tf_op jit(solution)/shard_map/all_to_all | solution.py:154
  515.4 20.5 %fusion.104 = f32[7,48,64]{2,1,0:T(8,128)S(1)} fusion(s32[15360]{0:T(1024)S(1)} %get-tuple-element.577, f32[7,15360]{1,0:T(8,128)S(1)} %pad_maximum_fusion.5, f32[15360,64]{0,1:T(8,128)} %fusion.70), kind=kOutput, calls=%fused_computation.237 | convolution fusion | flops 3971235840 | bytes 4509696 | tf_op jit(solution)/shard_map/sh,tsl->thl/dot_general | solution.py:162
  536.2 12.2 %fusion.62 = f32[6,15360]{1,0:T(8,128)S(1)} fusion(f32[6,48,64]{2,1,0:T(8,128)S(1)} %reshape.373, f32[15360,64]{0,1:T(8,128)} %fusion.70, s32[15360]{0:T(1024)S(1)} %get-tuple-element.577), kind=kOutput, calls=%fused_computation.205 | convolution fusion | flops 3409827840 | bytes 4435968 | tf_op jit(solution)/shard_map/sh,thl->tsl/dot_general | solution.py:168
  549.0 18.8 %all_to_all.31 = f32[6,32,480]{2,0,1:T(8,128)S(1)} all-to-all(f32[6,32,480]{2,0,1:T(8,128)S(1)} %copy.112), channel_id=1, replica_groups=mesh['sect'=2,'cols'=16] {'sect','cols'}, dimensions={1} | all-to-all | bytes 737280 | tf_op jit(solution)/shard_map/all_to_all | solution.py:175
  567.7 62.2 %fusion.52 = f32[6,12288]{1,0:T(8,128)S(1)} fusion(f32[12288,480]{0,1:T(8,128)} %compare_convert_fusion, s32[12288]{0:T(1024)S(1)} %bitcast.868, f32[6,32,480]{2,0,1:T(8,128)S(1)} %all_to_all.31), kind=kOutput, calls=%fused_computation.193 | convolution fusion | flops 13660643328 | bytes 24305664 | tf_op jit(solution)/shard_map/ed,tdr->ter/dot_general | solution.py:178
  630.0 4.9 convolution_bitcast_fusion
  634.9 1.2 div.210
  636.2 13.7 %all-reduce.8.cloned.1.call-done = f32[6,6144]{1,0:T(8,128)} async-done(((f32[6,6144]{1,0:T(8,128)}), f32[6,6144]{1,0:T(8,128)}) %all-reduce.8.cloned.1.call-update) | async-done | bytes 147472 | tf_op jit(solution)/shard_map/psum | solution.py:140
  650.8 3.3 conditional.6
  650.8 3.2 broadcast.139
  655.0 1.3 collective-permute-start.1
  656.3 38.9 %collective-permute-done.1 = f32[6,6144]{1,0:T(8,128)S(1)} collective-permute-done((f32[6,6144]{1,0:T(8,128)S(1)}, f32[6,6144]{1,0:T(8,128)S(1)}, u32[]{:S(2)}, u32[]{:S(2)}) %collective-permute-start.1) | collective-permute-done | bytes 147488 | tf_op jit(solution)/shard_map/ppermute | solution.py:17
  695.2 37.5 %conditional.7 = (f32[32,6,6144]{2,0,1:T(8,128)S(1)}) conditional(s32[]{:T(128)} %convert_element_type.30, (f32[32,6,6144]{2,1,0:T(8,128)}, f32[32,6144]{1,0:T(8,128)S(1)}, f32[6,6144]{1,0:T(8,128)S(1)}) %tuple.103, (f32[6,6144]{1,0:T(8,128)S(1)}, f32[31,6,6144]{2,1,0:T(8,128)}) %tuple.104), branch_computations={%region_22.25_spmd, %region_25.26_spmd} | conditional | flops 1179648 | bytes 23544292 | solution.py:208
  695.2 3.4 broadcast.141
  698.6 28.3 %while.62 = (s32[]{:T(128)}, f32[6,6144]{1,0:T(8,128)S(1)}, f32[4,8,6,6144]{3,2,1,0:T(8,128)}, f32[4,8,6,6144]{3,2,1,0:T(8,128)}, f32[4,8,6144]{2,1,0:T(8,128)S(...) while((s32[]{:T(128)}, f32[6,6144]{1,0:T(8,128)S(1)}, ...), condition=%wide.region_24.24_spmd, body=%wide.region_23.23_spmd.sunk | while | flops 884745 | bytes 9388377 | solution.py:43
  698.8 1.7 bitcast_dynamic-update-slice_fusion.83
  704.4 1.3 bitcast_dynamic-update-slice_fusion.91
  705.9 1.7 bitcast_dynamic-update-slice_fusion.83
  711.5 1.3 bitcast_dynamic-update-slice_fusion.91
  713.0 1.7 bitcast_dynamic-update-slice_fusion.83
  718.6 1.3 bitcast_dynamic-update-slice_fusion.91
  720.0 1.7 bitcast_dynamic-update-slice_fusion.83
  725.7 1.3 bitcast_dynamic-update-slice_fusion.91
  727.0 5.5 copy.115
  732.8 2.2 copy-done.2
  (182 shorter events, 62.7 us)
Async XLA Ops:
  7.2 144.2 %all-reduce.4.cloned.1.call-start = ((), (), s32[]{:S(2)}) async-start(), calls=%async_computation.4 | async-start | bytes 393216 | tf_op jit(solution)/shard_map/psum | solution.py:140
  7.2 61.0 %copy-start.3 = (s32[12288,1]{0,1:T(1,128)S(1)}, s32[12288,1]{0,1:T(1,128)}, u32[]{:S(2)}) copy-start(s32[12288,1]{0,1:T(1,128)} %param.35) | copy-start | bytes 147460
  66.1 30.0 %collective-permute-start = (f32[7,6144]{1,0:T(8,128)S(1)}, f32[7,6144]{1,0:T(8,128)S(1)}, u32[]{:S(2)}, u32[]{:S(2)}) collective-permute-start(f32[7,6144]{1,0:T(8,128)S(1)} %get-tuple-element.355), channel_id=1, source_target_pairs={{0,16},{1,17},{2,18},{3,19},{4,20},{5,21},{6,22},{7,23},{8,24},{9,... | collective-permute-start | bytes 516104 | tf_op jit(solution)/shard_map/ppermute | solution.py:17
  74.9 10.0 %copy-start.14 = (s32[1,48]{1,0:T(1,128)S(1)}, s32[1,48]{1,0:T(1,128)}, u32[]{:S(2)}) copy-start(s32[1,48]{1,0:T(1,128)} %param.33) | copy-start | bytes 580
  85.2 10.8 %copy-start.11 = (f32[12288]{0:T(1024)S(1)}, f32[12288]{0:T(1024)}, u32[]{:S(2)}) copy-start(f32[12288]{0:T(1024)} %param.37) | copy-start | bytes 147460
  85.2 10.8 %copy-start.12 = (f32[12288]{0:T(1024)S(1)}, f32[12288]{0:T(1024)}, u32[]{:S(2)}) copy-start(f32[12288]{0:T(1024)} %param.36) | copy-start | bytes 147460
  85.2 10.8 %copy-start.9 = (s32[15360]{0:T(1024)S(1)}, s32[15360]{0:T(1024)}, u32[]{:S(2)}) copy-start(s32[15360]{0:T(1024)} %param.38) | copy-start | bytes 184324
  85.2 10.8 %copy-start.10 = (s32[12288]{0:T(1024)S(1)}, s32[12288]{0:T(1024)}, u32[]{:S(2)}) copy-start(s32[12288]{0:T(1024)} %param.34) | copy-start | bytes 147460
  96.1 3.0 copy-start.13
  240.7 24.7 %copy-start.5 = (f32[15360]{0:T(1024)S(1)}, f32[15360]{0:T(1024)}, u32[]{:S(2)}) copy-start(f32[15360]{0:T(1024)} %param.39) | copy-start | bytes 184324
  241.8 22.8 %all-to-all-start = ((f32[7,32,480]{2,0,1:T(8,128)}), f32[7,32,480]{2,0,1:T(8,128)S(1)}, u32[]{:S(2)}, u32[]{:S(2)}) async-start(f32[7,32,480]{2,0,1:T(8,128)} %copy.105), calls=%async_computation | async-start | bytes 1048576 | tf_op jit(solution)/shard_map/all_to_all | solution.py:154
  265.6 20.8 %copy-start.6 = (f32[3072]{0:T(1024)S(1)}, f32[3072]{0:T(1024)}, u32[]{:S(2)}) copy-start(f32[3072]{0:T(1024)} %param.32) | copy-start | bytes 36868
  265.6 20.8 %copy-start.8 = (f32[6,3072]{1,0:T(8,128)S(1)}, f32[6,3072]{1,0:T(8,128)}, u32[]{:S(2)}) copy-start(f32[6,3072]{1,0:T(8,128)} %param.31) | copy-start | bytes 221188
  300.2 19.4 %all-to-all-start.1 = ((f32[6,32,480]{2,0,1:T(8,128)}), f32[6,32,480]{2,0,1:T(8,128)S(1)}, u32[]{:S(2)}, u32[]{:S(2)}) async-start(f32[6,32,480]{2,0,1:T(8,128)} %copy.107), calls=%async_computation.1 | async-start | bytes 1048576 | tf_op jit(solution)/shard_map/all_to_all | solution.py:175
  302.9 98.9 %all-reduce.6.cloned.1.call-start = ((), (), s32[]{:S(2)}) async-start(), calls=%async_computation.5 | async-start | bytes 393216 | tf_op jit(solution)/shard_map/psum | solution.py:140
  302.9 98.8 %copy-start.7 = (f32[6,6144]{1,0:T(8,128)S(1)}, f32[6,6144]{1,0:T(8,128)}, u32[]{:S(2)}) copy-start(f32[6,6144]{1,0:T(8,128)} %all-reduce.4.cloned.1.call-done) | copy-start | bytes 442372
  386.8 263.0 %all-reduce.8.cloned.1.call-start = ((), (), s32[]{:S(2)}) async-start(), calls=%async_computation.6 | async-start | bytes 393216 | tf_op jit(solution)/shard_map/psum | solution.py:140
  536.1 12.3 %copy-start.4 = (f32[6,3072]{1,0:T(8,128)}, f32[6,3072]{1,0:T(8,128)S(1)}, u32[]{:S(2)}) copy-start(f32[6,3072]{1,0:T(8,128)S(1)} %add_divide_fusion) | copy-start | bytes 221188
  567.7 67.2 %copy-start.1 = (f32[32,6144]{1,0:T(8,128)S(1)}, f32[32,6144]{1,0:T(8,128)}, u32[]{:S(2)}) copy-start(f32[32,6144]{1,0:T(8,128)} %param.29) | copy-start | bytes 2359300
  655.0 40.2 %collective-permute-start.1 = (f32[6,6144]{1,0:T(8,128)S(1)}, f32[6,6144]{1,0:T(8,128)S(1)}, u32[]{:S(2)}, u32[]{:S(2)}) collective-permute-start(f32[6,6144]{1,0:T(8,128)S(1)} %slice_bitcast_fusion.1), channel_id=1, source_target_pairs={{16,0},{17,1},{18,2},{19,3},{20,4},{21,5},{22,6},{23,7},{24,8},{25... | collective-permute-start | bytes 442376 | tf_op jit(solution)/shard_map/ppermute | solution.py:17
  732.7 2.2 copy-start.2
Sparse Core Ops, SparseCore 0:
  99.3 52.0 all-reduce.3
  386.9 14.7 all-reduce.5
  635.0 14.7 all-reduce.7
where the time goes:
time: 749 us; the launch traced here: 742 us
  matrix products  379 us (51%)
  waiting for transfers between devices  116 us (15%)
  other arithmetic  80.2 us (11%)
  blocking collectives  76.2 us (10%)
  local copies, waits for them, and re-layouts  63.1 us (8%)
  between operations  14.8 us (2%)
  starting transfers between devices  11.5 us (2%)
    dot_general x2, matrix products, body(): jnp.einsum('ed,ter->tdr', owner_flat, spread, precision=highest)  167 us
    dot_general x2, matrix products, body(): jnp.einsum('ed,tdr->ter', owner_flat, returned.reshape(tracers, devices,...  124 us
    while x44, other arithmetic  47.5 us
    psum x3, waiting for transfers between devices, body(): lax.psum((flux_part, resid_share, slope_share), 'sect')  45.6 us
    dot_general x2, matrix products, body(): jnp.einsum('sh,tsl->thl', group_map, placed, precision=highest)  41 us
    ppermute x2, waiting for transfers between devices, shifted(): lax.ppermute(value, axis, [(source, source + steps) for source in range(i...  38.9 us
    psum x1, blocking collectives, body(): lax.psum((flux_part, resid_share, slope_share), 'sect')  34.9 us
    dot_general x2, matrix products, body(): jnp.einsum('sh,thl->tsl', group_map, sea.reshape(tracers, groups, cell_gr...  24.6 us
  transfers between devices with their start and end apart: 7, of which 6 were waited for; matrix products, arithmetic and copies ran while one was open for 4% of the time, Pallas kernels for 0%

commit v1 on v0

v1 whole, which is shorter than its diff:
```python
import functools

import jax
import jax.numpy as jnp
from jax import lax
from jax.experimental import pallas as pl
from jax.experimental.pallas import tpu as pltpu
from jax.sharding import PartitionSpec as P

BLOCK_COLS = 128
BLOCK_SLOTS = 256
SUBSTEPS = 2
LANES = 128
COL_TILE = 1024
PARAMS = pltpu.CompilerParams(vmem_limit_bytes=40 * 1024 * 1024)


def split(value):
    high = value.astype(jnp.bfloat16).astype(jnp.float32)
    return high, value - high


def pair(ref, i):
    return jnp.concatenate([ref[pl.ds(2 * i, 1), :], ref[pl.ds(2 * i + 1, 1), :]], axis=1)


def wide(ref, i):
    return jnp.concatenate([ref[2 * i], ref[2 * i + 1]], axis=1)


def onehot(index, count):
    return lax.broadcasted_iota(jnp.int32, (count, index.shape[1]), 0) == index


def lanes_map(lane):
    return jnp.where(onehot(lane, LANES), 1.0, 0.0).astype(jnp.bfloat16)


def scatter_step(acc, values, row, lane, rows):
    mask = onehot(row, rows)
    high, low = split(values)
    left = [
        jnp.concatenate(
            [jnp.where(mask, part[q : q + 1], 0.0) for q in range(values.shape[0])], axis=0
        ).astype(jnp.bfloat16)
        for part in (high, low)
    ]
    lane_hot = lanes_map(lane)
    acc[...] += lax.dot_general(
        jnp.concatenate(left, axis=1),
        jnp.concatenate([lane_hot, lane_hot], axis=1),
        (((1,), (1,)), ((), ())),
        preferred_element_type=jnp.float32,
    )


def table_of(value):
    high, low = split(value)
    return jnp.concatenate([high, low], axis=1).astype(jnp.bfloat16)


def gather_step(table, row, lane, rows, count):
    lane_hot = lanes_map(lane)
    picked = jnp.dot(
        table, jnp.concatenate([lane_hot, lane_hot], axis=0), preferred_element_type=jnp.float32
    )
    mask = onehot(row, rows)
    return jnp.concatenate(
        [
            jnp.sum(jnp.where(mask, picked[q * rows : (q + 1) * rows], 0.0), axis=0, keepdims=True)
            for q in range(count)
        ],
        axis=0,
    )


def setup_kernel(devices, cap_rows, owner, column, coef, weight, counts, out, acc, offset):
    acc[...] = jnp.zeros_like(acc)
    offset[...] = jnp.zeros_like(offset)
    later = (
        lax.broadcasted_iota(jnp.int32, (BLOCK_SLOTS, BLOCK_SLOTS), 0)
        <= lax.broadcasted_iota(jnp.int32, (BLOCK_SLOTS, BLOCK_SLOTS), 1)
    )
    later = jnp.where(later, 1.0, 0.0).astype(jnp.bfloat16)
    within = lax.broadcasted_iota(jnp.int32, (1, BLOCK_SLOTS), 1)

    def block(i, _):
        own = pair(owner, i)
        named = jnp.where(onehot(own, devices), 1.0, 0.0)
        running = (
            jnp.dot(named.astype(jnp.bfloat16), later, preferred_element_type=jnp.float32)
            + offset[:, 0:1]
        )
        rank = (jnp.sum(named * running, axis=0, keepdims=True) - 1.0).astype(jnp.int32)
        offset[...] += jnp.broadcast_to(jnp.sum(named, axis=1, keepdims=True), offset.shape)
        live = within < counts[pl.ds(i, 1), 0:1]
        gain = jnp.where(live, pair(coef, i), 0.0)
        flow = pair(weight, i) * gain
        gain_high, gain_low = split(gain)
        flow_high, flow_low = split(flow)
        values = jnp.concatenate(
            [
                jnp.full((1, BLOCK_SLOTS), i, jnp.int32).astype(jnp.float32),
                pair(column, i).astype(jnp.float32),
                gain_high,
                gain_low,
                flow_high,
                flow_low,
            ],
            axis=0,
        )
        mask = onehot(own * cap_rows + rank // LANES, LANES)
        left = jnp.concatenate(
            [jnp.where(mask, values[q : q + 1], 0.0) for q in range(6)], axis=0
        ).astype(jnp.bfloat16)
        acc[...] += lax.dot_general(
            left,
            lanes_map(rank % LANES),
            (((1,), (1,)), ((), ())),
            preferred_element_type=jnp.float32,
        )
        return 0

    lax.fori_loop(0, owner.shape[0] // 2, block, 0)
    out[0] = acc[0:128]
    out[1] = acc[128:256]
    out[2] = acc[256:384] + acc[384:512]
    out[3] = acc[512:640] + acc[640:768]


def setup(owner, column, coef, weight, counts, devices, cap_rows):
    return pl.pallas_call(
        functools.partial(setup_kernel, devices, cap_rows),
        out_shape=jax.ShapeDtypeStruct((4, LANES, LANES), jnp.float32),
        scratch_shapes=[
            pltpu.VMEM((6 * LANES, LANES), jnp.float32),
            pltpu.VMEM((devices, LANES), jnp.float32),
        ],
        compiler_params=PARAMS,
    )(owner, column, coef, weight, counts)


def level_down(mix, air, k, under, carried):
    coupling = mix[k : k + 1, :]
    inverse = 1.0 / (1.0 + coupling + under)
    part = (air[k] + carried) * inverse
    ratio = coupling * inverse
    return part, ratio, inverse, ratio * (1.0 + under), coupling * part


def descend_end_kernel(air, mix, end):
    under = jnp.zeros((1, end.shape[1]), jnp.float32)
    carried = jnp.zeros((air.shape[1], end.shape[1]), jnp.float32)
    for k in range(air.shape[0]):
        _, _, _, under, carried = level_down(mix, air, k, under, carried)
    end[...] = jnp.concatenate([carried, under], axis=0)


def descend_end(air, mix):
    levels, tracers, columns = air.shape
    return pl.pallas_call(
        descend_end_kernel,
        grid=(columns // COL_TILE,),
        in_specs=[
            pl.BlockSpec((levels, tracers, COL_TILE), lambda j: (0, 0, j)),
            pl.BlockSpec((levels, COL_TILE), lambda j: (0, j)),
        ],
        out_specs=pl.BlockSpec((tracers + 1, COL_TILE), lambda j: (0, j)),
        out_shape=jax.ShapeDtypeStruct((tracers + 1, columns), jnp.float32),
        compiler_params=PARAMS,
    )(air, mix)


def descend_kernel(air, mix, start, last, parts, ratios, ends):
    levels, tracers, _ = air.shape
    carried = start[0:tracers, :]
    under = start[tracers : tracers + 1, :]
    for k in range(levels):
        part, ratio, inverse, under, carried = level_down(mix, air, k, under, carried)
        parts[k] = part
        if k == levels - 1:
            ratio = last[...] * inverse
        ratios[k : k + 1, :] = ratio
    value, factor = part, ratio
    ends[0, 0:tracers, :] = part
    ends[0, tracers : tracers + 1, :] = ratio
    for k in range(levels - 2, -1, -1):
        ratio = ratios[k : k + 1, :]
        value = parts[k] + ratio * value
        factor = ratio * factor
    ends[1, 0:tracers, :] = value
    ends[1, tracers : tracers + 1, :] = factor


def descend(air, mix, start, last):
    levels, tracers, columns = air.shape
    return pl.pallas_call(
        descend_kernel,
        grid=(columns // COL_TILE,),
        in_specs=[
            pl.BlockSpec((levels, tracers, COL_TILE), lambda j: (0, 0, j)),
            pl.BlockSpec((levels, COL_TILE), lambda j: (0, j)),
            pl.BlockSpec((tracers + 1, COL_TILE), lambda j: (0, j)),
            pl.BlockSpec((1, COL_TILE), lambda j: (0, j)),
        ],
        out_specs=[
            pl.BlockSpec((levels, tracers, COL_TILE), lambda j: (0, 0, j)),
            pl.BlockSpec((levels, COL_TILE), lambda j: (0, j)),
            pl.BlockSpec((2, tracers + 1, COL_TILE), lambda j: (0, 0, j)),
        ],
        out_shape=[
            jax.ShapeDtypeStruct(air.shape, jnp.float32),
            jax.ShapeDtypeStruct(mix.shape, jnp.float32),
            jax.ShapeDtypeStruct((2, tracers + 1, columns), jnp.float32),
        ],
        compiler_params=PARAMS,
    )(air, mix, start, last)


def ascend_kernel(parts, ratios, below, out):
    value = below[...]
    for k in range(parts.shape[0] - 1, -1, -1):
        value = parts[k] + ratios[k : k + 1, :] * value
        out[k] = value


def ascend(parts, ratios, below):
    levels, tracers, columns = parts.shape
    return pl.pallas_call(
        ascend_kernel,
        grid=(columns // COL_TILE,),
        in_specs=[
            pl.BlockSpec((levels, tracers, COL_TILE), lambda j: (0, 0, j)),
            pl.BlockSpec((levels, COL_TILE), lambda j: (0, j)),
            pl.BlockSpec((tracers, COL_TILE), lambda j: (0, j)),
        ],
        out_specs=pl.BlockSpec((levels, tracers, COL_TILE), lambda j: (0, 0, j)),
        out_shape=jax.ShapeDtypeStruct(parts.shape, jnp.float32),
        compiler_params=PARAMS,
    )(parts, ratios, below)


def send_kernel(tracers, resid, slope, flux, other, block, column, gain, out):
    rows = slope.shape[0]
    flux_col = flux[...] + other[...]
    bottom = resid[...] + jnp.concatenate([slope[...]] * tracers, axis=0) * flux_col
    table = table_of(bottom)

    def step(i, _):
        at = gather_step(table, pair(block, i), pair(column, i), rows, tracers)
        sent = jnp.concatenate(
            [at, pair(gain, i), jnp.zeros((7 - tracers, 2 * LANES), jnp.float32)], axis=0
        )
        out[2 * i] = sent[:, 0:LANES]
        out[2 * i + 1] = sent[:, LANES:]
        return 0

    lax.fori_loop(0, block.shape[0] // 2, step, 0, unroll=4)


def send(tracers, resid, slope, flux, other, block, column, gain):
    return pl.pallas_call(
        functools.partial(send_kernel, tracers),
        out_shape=jax.ShapeDtypeStruct((block.shape[0], 8, LANES), jnp.float32),
        compiler_params=PARAMS,
    )(resid, slope, flux, other, block, column, gain)


def surface_kernel(tracers, arrived, frac, row, lane, sea, rate, out, sea_new, acc):
    rows = rate.shape[0]
    acc[...] = jnp.zeros_like(acc)

    def gathering(i, _):
        came = wide(arrived, i)
        coupling = came[tracers : tracers + 1] * pair(frac, i)
        values = jnp.concatenate([came[0:tracers] * coupling, coupling], axis=0)
        scatter_step(acc, values, pair(row, i), pair(lane, i), rows)
        return 0

    lax.fori_loop(0, row.shape[0] // 2, gathering, 0, unroll=4)
    strength = rate[...]
    inverse = 1.0 / (1.0 + strength * acc[tracers * rows : (tracers + 1) * rows])
    for q in range(tracers):
        here = slice(q * rows, (q + 1) * rows)
        sea_new[here] = (sea[here] + strength * acc[here]) * inverse
    table = table_of(sea_new[...])

    def returning(i, _):
        seen = gather_step(table, pair(row, i), pair(lane, i), rows, tracers)
        sent = jnp.concatenate([seen, jnp.zeros((8 - tracers, 2 * LANES), jnp.float32)], axis=0)
        out[2 * i] = sent[:, 0:LANES]
        out[2 * i + 1] = sent[:, LANES:]
        return 0

    lax.fori_loop(0, row.shape[0] // 2, returning, 0, unroll=4)


def surface(tracers, arrived, frac, row, lane, sea, rate):
    return pl.pallas_call(
        functools.partial(surface_kernel, tracers),
        out_shape=[
            jax.ShapeDtypeStruct(arrived.shape, jnp.float32),
            jax.ShapeDtypeStruct(sea.shape, jnp.float32),
        ],
        scratch_shapes=[pltpu.VMEM(((tracers + 1) * rate.shape[0], LANES), jnp.float32)],
        compiler_params=PARAMS,
    )(arrived, frac, row, lane, sea, rate)


def collect_kernel(tracers, returned, sent, flow, block, column, flux):
    rows = flux.shape[0] // tracers
    flux[...] = jnp.zeros_like(flux)

    def step(i, _):
        values = (wide(returned, i) - wide(sent, i))[0:tracers] * pair(flow, i)
        scatter_step(flux, values, pair(block, i), pair(column, i), rows)
        return 0

    lax.fori_loop(0, block.shape[0] // 2, step, 0, unroll=4)


def collect(tracers, rows, returned, sent, flow, block, column):
    return pl.pallas_call(
        functools.partial(collect_kernel, tracers),
        out_shape=jax.ShapeDtypeStruct((tracers * rows, LANES), jnp.float32),
        compiler_params=PARAMS,
    )(returned, sent, flow, block, column)


def body(
    air_state,
    mix_coef,
    flux_scale,
    sea_state,
    sea_rate,
    block_counts,
    cell_column,
    cell_owner,
    cell_coef,
    cell_weight,
    slot_cell,
    slot_frac,
):
    levels, tracers, columns = air_state.shape
    is_lower = lax.axis_index("sect") == 1
    devices = lax.axis_size("sect") * lax.axis_size("cols")
    rows = columns // BLOCK_COLS
    surf_cells = sea_state.shape[1]
    surf_rows = surf_cells // LANES
    capacity = slot_cell.shape[0] // devices
    cap_rows = -(-capacity // LANES)
    padding = ((0, 0), (0, cap_rows * LANES - capacity))

    handed = lax.ppermute(descend_end(air_state, mix_coef), "sect", [(0, 1)])
    slots = setup(
        cell_owner.reshape(-1, LANES),
        cell_column.reshape(-1, LANES),
        cell_coef.reshape(-1, LANES),
        cell_weight.reshape(-1, LANES),
        jnp.broadcast_to(block_counts.reshape(-1, 1), (rows, LANES)),
        devices,
        cap_rows,
    )
    block = slots[0].astype(jnp.int32)
    column = slots[1].astype(jnp.int32)
    gain, flow = slots[2], slots[3]
    cell = jnp.pad(slot_cell.reshape(devices, capacity), padding).reshape(-1, LANES)
    frac = jnp.pad(slot_frac.reshape(devices, capacity), padding).reshape(-1, LANES)
    row, lane = cell // LANES, cell % LANES

    last = jnp.where(is_lower, flux_scale, mix_coef[-1])[None]
    parts, ratios, ends = descend(air_state, mix_coef, handed, last)
    received = lax.ppermute(ends, "sect", [(1, 0)])
    low = jnp.where(is_lower, ends, received)
    resid = low[0, :tracers].reshape(tracers * rows, LANES)
    slope = low[0, tracers].reshape(rows, LANES)

    sea = sea_state.reshape(tracers * surf_rows, LANES)
    rate = sea_rate.reshape(surf_rows, LANES)
    flux = other = jnp.zeros((tracers * rows, LANES), jnp.float32)
    for _ in range(SUBSTEPS):
        sent = send(tracers, resid, slope, flux, other, block, column, gain)
        arrived = lax.all_to_all(sent, ("sect", "cols"), split_axis=0, concat_axis=0, tiled=True)
        back, sea = surface(tracers, arrived, frac, row, lane, sea, rate)
        returned = lax.all_to_all(back, ("sect", "cols"), split_axis=0, concat_axis=0, tiled=True)
        flux = collect(tracers, rows, returned, sent, flow, block, column)
        other = lax.ppermute(flux, "sect", [(0, 1), (1, 0)])
    flux_col = (flux + other).reshape(tracers, columns)
    below = jnp.where(is_lower, flux_col, low[1, :tracers] + low[1, tracers] * flux_col)
    return (ascend(parts, ratios, below), sea.reshape(tracers, surf_cells))


def solution(mesh):
    return jax.shard_map(
        body,
        mesh=mesh,
        in_specs=(
            P("sect", None, "cols"),
            P("sect", "cols"),
            P("cols"),
            P(None, ("sect", "cols")),
            P(("sect", "cols")),
            P(("sect", "cols"), None),
            P(("sect", "cols")),
            P(("sect", "cols"), None),
            P(("sect", "cols")),
            P(("sect", "cols")),
            P(("sect", "cols")),
            P(("sect", "cols")),
        ),
        out_specs=(P("sect", None, "cols"), P(None, ("sect", "cols"))),
        check_vma=False,
    )
```

time: 749 us -> 190 us (0.25)
  matrix products: 379 us -> 0 us
  waiting for transfers between devices: 116 us -> 19.5 us
  Pallas kernels: 0 us -> 82.6 us
  other arithmetic: 80.2 us -> 0.21 us
  local copies, waits for them, and re-layouts: 63.1 us -> 19.4 us
  blocking collectives: 76.2 us -> 55.7 us
  between operations: 14.8 us -> 1.03 us
    dot_general x13 -> x0, matrix products: 379 us -> none  [the longest x2 167 us: body(): jnp.einsum('ed,ter->tdr', owner_flat, spread, precision=highest)]
    pallas_call x0 -> x10, Pallas kernels: none -> 82.6 us  [the longest x1 22 us: setup(): pl.pallas_call(functools.partial(setup_kernel, devices, cap_rows), out_sh...]
    while x44 -> x0, other arithmetic: 47.5 us -> none
    psum x3 -> x0, waiting for transfers between devices: 45.6 us -> none  [body(): lax.psum((flux_part, resid_share, slope_share), 'sect')]
    ppermute x2 -> x4, waiting for transfers between devices: 38.9 us -> 3.04 us  [the longest x2 2.06 us: body(): other = lax.ppermute(flux, 'sect', [(0, 1), (1, 0)])]
    psum x1 -> x0, blocking collectives: 34.9 us -> none  [body(): lax.psum((flux_part, resid_share, slope_share), 'sect')]
    unnamed x30, local copies, waits for them, and re-layouts: 2.8 us -> 18.3 us
    all_to_all x2 -> x1, waiting for transfers between devices: 31.3 us -> 16.5 us  [body(): lax.all_to_all(sent, ('sect', 'cols'), split_axis=0, concat_axis=0, tiled...]
  transfers between devices with their start and end apart: 7 -> 5, of which waited for: 6 -> 4; matrix products, arithmetic and copies ran while one was open for 4% -> 1% of each run, Pallas kernels for 0% -> 12%
where the time goes in v1:
time: 190 us
  Pallas kernels  82.6 us (43%)
  blocking collectives  55.7 us (29%)
  waiting for transfers between devices  19.5 us (10%)
  local copies, waits for them, and re-layouts  19.4 us (10%)
  starting transfers between devices  11.2 us (6%)
    all_to_all x2, blocking collectives, body(): lax.all_to_all(back, ('sect', 'cols'), split_axis=0, concat_axis=0, tiled...  37.1 us
    pallas_call x1, Pallas kernels, setup(): pl.pallas_call(functools.partial(setup_kernel, devices, cap_rows), out_sh...  22 us
    pallas_call x2, Pallas kernels, surface(): pl.pallas_call(functools.partial(surface_kernel, tracers), out_shape=[jax...  21.3 us
    all_to_all x1, blocking collectives, body(): lax.all_to_all(sent, ('sect', 'cols'), split_axis=0, concat_axis=0, tiled...  18.6 us
    unnamed x30, local copies, waits for them, and re-layouts  18.3 us
    all_to_all x1, waiting for transfers between devices, body(): lax.all_to_all(sent, ('sect', 'cols'), split_axis=0, concat_axis=0, tiled...  16.5 us
    pallas_call x2, Pallas kernels, collect(): pl.pallas_call(functools.partial(collect_kernel, tracers), out_shape=jax....  16.1 us
    pallas_call x2, Pallas kernels, send(): pl.pallas_call(functools.partial(send_kernel, tracers), out_shape=jax.Sha...  12.5 us
  transfers between devices with their start and end apart: 5, of which 4 were waited for; matrix products, arithmetic and copies ran while one was open for 1% of the time, Pallas kernels for 12%

profile of v1, /device:TPU:0, one launch (start us, length us, event | category | flops | bytes accessed | tf_op | source)
XLA Modules:
  0.0 189.6 jit_solution(13088362873658698853)
XLA Ops:
  0.6 0.0 copy-start.3
  0.6 5.2 %copy.18.air = f32[32,6,6144]{2,1,0:T(8,128)S(1)} copy(f32[32,6,6144]{2,0,1:T(8,128)} %param.12) | data formatting | bytes 9437184 | tf_op args[0]
  5.9 0.0 copy-done.3
  5.9 0.0 copy-start.12
  5.9 0.0 copy-start.13
  5.9 0.0 copy-start.4
  5.9 0.0 copy-start.5
  5.9 0.0 copy-start.6
  6.0 0.0 copy-start.7
  6.0 2.7 %shard_map.131 = f32[7,6144]{1,0:T(8,128)S(1)} custom-call(f32[32,6,6144]{2,1,0:T(8,128)S(1)} %copy.18.air, f32[32,6144]{1,0:T(8,128)S(1)} %copy-done.3), custom_call_target="tpu_custom_call" | custom-call | tf_op jit(solution)/shard_map/pallas_call | solution.py:161
  8.7 0.0 copy-start
  8.7 2.6 %copy-done = f32[32,6,6144]{2,1,0:T(8,128)} copy-done((f32[32,6,6144]{2,1,0:T(8,128)}, f32[32,6,6144]{2,1,0:T(8,128)S(1)}, u32[]{:S(2)}) %copy-start) | copy-done | bytes 4718616
  11.4 2.4 %collective-permute-start = (f32[7,6144]{1,0:T(8,128)S(1)}, f32[7,6144]{1,0:T(8,128)S(1)}, u32[]{:S(2)}, u32[]{:S(2)}) collective-permute-start(f32[7,6144]{1,0:T(8,128)S(1)} %shard_map.131), channel_id=1, source_target_pairs={{0,16},{1,17},{2,18},{3,19},{4,20},{5,21},{6,22},{7,23},{8,24},{9,... | collective-permute-start | bytes 516104 | tf_op jit(solution)/shard_map/ppermute | solution.py:354
  13.8 0.0 copy-done.12
  13.8 1.0 collective-permute-done.start
  14.8 0.0 copy-start.10
  14.8 0.0 copy-start.11
  14.8 0.0 copy-start.9
  14.8 0.0 copy-start.8
  14.8 6.0 %shard_map.132 = (f32[32,6,6144]{2,1,0:T(8,128)S(1)}, f32[32,6144]{1,0:T(8,128)S(1)}, f32[2,7,6144]{2,1,0:T(8,128)S(1)}) custom-call(f32[32,6,6144]{2,1,0:T(8,128)} %copy-done, f32[32,6144]{1,0:T(8,128)S(1)} %copy-done.3, f32[7,6144]{1,0:T(8,128)S(1)} %collective-permute-done.start, f32[1,6144]{1,0:T(1,128)S(1)} %bitcast.26), custom_call_target="tpu_custom_call" | custom-call | tf_op jit(solution)/shard_map/pallas_call | solution.py:197
  20.8 0.0 copy-start.1
  20.8 2.6 %copy-done.1 = f32[32,6,6144]{2,1,0:T(8,128)} copy-done((f32[32,6,6144]{2,1,0:T(8,128)}, f32[32,6,6144]{2,1,0:T(8,128)S(1)}, u32[]{:S(2)}) %copy-start.1) | copy-done | bytes 4718616
  23.4 1.3 collective-permute-start.1
  24.7 0.0 copy-done.13
  24.7 0.1 broadcast_in_dim.16.counts
  24.8 0.0 copy-done.4
  24.8 0.0 copy-done.5
  24.8 0.0 copy-done.6
  24.8 0.0 copy-done.7
  24.8 22.0 %shard_map.133 = f32[4,128,128]{2,1,0:T(8,128)S(1)} custom-call(s32[96,128]{1,0:T(8,128)S(1)} %bitcast.27, s32[96,128]{1,0:T(8,128)S(1)} %bitcast.28, f32[96,128]{1,0:T(8,128)S(1)} %bitcast.29, f32[96,128]{1,0:T(8,128)S(1)} %bitcast.30, s32[48,128]{1,0:T(8,128)S(1)} %broadcast_in_dim.16.counts), custom_call_target="tpu_custom_call" | custom-call | tf_op jit(solution)/shard_map/pallas_call | solution.py:132
  46.8 0.0 collective-permute-done.1
  46.8 0.1 broadcast_select_fusion
  46.9 0.1 fusion.6
  47.1 6.7 %shard_map.134.sent = f32[128,8,128]{2,1,0:T(8,128)} custom-call(f32[288,128]{1,0:T(8,128)S(1)} %reshape_squeeze.6.resid, f32[48,128]{1,0:T(8,128)S(1)} %bitcast.24, f32[288,128]{1,0:T(8,128)S(1)} %broadcast_in_dim.14.flux.other, f32[288,128]{1,0:T(8,128)S(1)} %broadcast_in_dim.14.flux.other, s32[128,128]{1,0:T(8,128)S(1)} %get-tuple-element.25.block, ...), custom_call_target="tpu_custom_call" | custom-call | tf_op jit(solution)/shard_map/pallas_call | solution.py:262
  53.7 7.4 %all-to-all-start = ((f32[128,8,128]{2,1,0:T(8,128)}), f32[128,8,128]{2,1,0:T(8,128)S(1)}, u32[]{:S(2)}, u32[]{:S(2)}) async-start(f32[128,8,128]{2,1,0:T(8,128)} %shard_map.134.sent), calls=%async_computation | async-start | bytes 1048576 | tf_op jit(solution)/shard_map/all_to_all | solution.py:383
  61.1 0.0 copy-done.10
  61.1 0.1 reshape.51
  61.3 0.0 copy-done.11
  61.3 0.1 reshape.49
  61.4 0.0 copy-done.9
  61.4 0.1 add_select_fusion
  61.5 16.5 %all-to-all-done.arrived = f32[128,8,128]{2,1,0:T(8,128)S(1)} async-done(((f32[128,8,128]{2,1,0:T(8,128)}), f32[128,8,128]{2,1,0:T(8,128)S(1)}, u32[]{:S(2)}, u32[]{:S(2)}) %all-to-all-start) | async-done | bytes 524320 | tf_op jit(solution)/shard_map/all_to_all | solution.py:383
  78.0 0.0 copy-done.8
  78.0 10.7 %shard_map.135 = (f32[128,8,128]{2,1,0:T(8,128)S(1)}, f32[144,128]{1,0:T(8,128)S(1)}) custom-call(f32[128,8,128]{2,1,0:T(8,128)S(1)} %all-to-all-done.arrived, f32[128,128]{1,0:T(8,128)S(1)} %reshape.50.frac, s32[128,128]{1,0:T(8,128)S(1)} %get-tuple-element.27.row, s32[128,128]{1,0:T(8,128)S(1)} %get-tuple-element.26.lane, f32[144,128]{1,0:T(8,128)S(1)} %reshape.53.sea, ...), custom_call_target="tpu_custom_call" | custom-call | tf_op jit(solution)/shard_map/pallas_call | solution.py:299
  88.6 18.6 %all_to_all.20.returned = f32[128,8,128]{2,1,0:T(8,128)S(1)} all-to-all(f32[128,8,128]{2,1,0:T(8,128)S(1)} %get-tuple-element.12), channel_id=1, replica_groups=mesh['sect'=2,'cols'=16] {'sect','cols'}, dimensions={0} | all-to-all | bytes 1048576 | tf_op jit(solution)/shard_map/all_to_all | solution.py:385
  107.2 8.6 %shard_map.136.flux = f32[288,128]{1,0:T(8,128)S(1)} custom-call(f32[128,8,128]{2,1,0:T(8,128)S(1)} %all_to_all.20.returned, f32[128,8,128]{2,1,0:T(8,128)} %shard_map.134.sent, f32[128,128]{1,0:T(8,128)S(1)} %get-tuple-element.22.flow, s32[128,128]{1,0:T(8,128)S(1)} %get-tuple-element.25.block, s32[128,128]{1,0:T(8,128)S(1)} %get-tuple-element.24.column), custom_call_target="tpu_custom_call" | custom-call | tf_op jit(solution)/shard_map/pallas_call | solution.py:323
  115.8 0.1 collective-permute-start.2
  115.9 1.4 collective-permute-done.2.other
  117.2 5.9 %shard_map.137.sent = f32[128,8,128]{2,1,0:T(8,128)S(1)} custom-call(f32[288,128]{1,0:T(8,128)S(1)} %reshape_squeeze.6.resid, f32[48,128]{1,0:T(8,128)S(1)} %bitcast.25, f32[288,128]{1,0:T(8,128)S(1)} %shard_map.136.flux, f32[288,128]{1,0:T(8,128)S(1)} %collective-permute-done.2.other, s32[128,128]{1,0:T(8,128)S(1)} %get-tuple-element.25.block, ...), custom_call_target="tpu_custom_call" | custom-call | tf_op jit(solution)/shard_map/pallas_call | solution.py:262
  123.1 18.6 %all_to_all.21.arrived = f32[128,8,128]{2,1,0:T(8,128)S(1)} all-to-all(f32[128,8,128]{2,1,0:T(8,128)S(1)} %shard_map.137.sent), channel_id=1, replica_groups=mesh['sect'=2,'cols'=16] {'sect','cols'}, dimensions={0} | all-to-all | bytes 1048576 | tf_op jit(solution)/shard_map/all_to_all | solution.py:383
  141.6 10.7 %shard_map.138 = (f32[128,8,128]{2,1,0:T(8,128)S(1)}, f32[144,128]{1,0:T(8,128)S(1)}) custom-call(f32[128,8,128]{2,1,0:T(8,128)S(1)} %all_to_all.21.arrived, f32[128,128]{1,0:T(8,128)S(1)} %reshape.50.frac, s32[128,128]{1,0:T(8,128)S(1)} %get-tuple-element.27.row, s32[128,128]{1,0:T(8,128)S(1)} %get-tuple-element.26.lane, ...), custom_call_target="tpu_custom_call" | custom-call | tf_op jit(solution)/shard_map/pallas_call | solution.py:299
  152.3 18.6 %all_to_all.22.returned = f32[128,8,128]{2,1,0:T(8,128)S(1)} all-to-all(f32[128,8,128]{2,1,0:T(8,128)S(1)} %get-tuple-element.14), channel_id=1, replica_groups=mesh['sect'=2,'cols'=16] {'sect','cols'}, dimensions={0} | all-to-all | bytes 1048576 | tf_op jit(solution)/shard_map/all_to_all | solution.py:385
  170.9 7.6 %shard_map.139 = f32[288,128]{1,0:T(8,128)S(1)} custom-call(f32[128,8,128]{2,1,0:T(8,128)S(1)} %all_to_all.22.returned, f32[128,8,128]{2,1,0:T(8,128)S(1)} %shard_map.137.sent, f32[128,128]{1,0:T(8,128)S(1)} %get-tuple-element.22.flow, s32[128,128]{1,0:T(8,128)S(1)} %get-tuple-element.25.block, s32[128,128]{1,0:T(8,128)S(1)} %get-tuple-element.24.column), custom_call_target="tpu_custom_call" | custom-call | tf_op jit(solution)/shard_map/pallas_call | solution.py:323
  178.4 0.1 collective-permute-start.3
  178.5 0.7 reshape.56
  179.2 0.7 collective-permute-done.3
  180.0 0.0 copy-start.2
  180.0 2.8 %copy-done.2 = f32[32,6,6144]{2,1,0:T(8,128)S(1)} copy-done((f32[32,6,6144]{2,1,0:T(8,128)S(1)}, f32[32,6,6144]{2,1,0:T(8,128)}, u32[]{:S(2)}) %copy-start.2) | copy-done | bytes 4718616
  182.8 1.9 %shard_map.140 = f32[32,6,6144]{2,1,0:T(8,128)S(1)} custom-call(f32[32,6,6144]{2,1,0:T(8,128)S(1)} %copy-done.2, f32[32,6144]{1,0:T(8,128)S(1)} %get-tuple-element.10.ratios, f32[6,6144]{1,0:T(8,128)S(1)} %fusion.1.below), custom_call_target="tpu_custom_call" | custom-call | tf_op jit(solution)/shard_map/pallas_call | solution.py:229
  184.7 4.9 %copy.19 = f32[32,6,6144]{2,0,1:T(8,128)} copy(f32[32,6,6144]{2,1,0:T(8,128)S(1)} %shard_map.140) | data formatting | bytes 9437184
  (14 shorter events, 0.3 us)
Async XLA Ops:
  0.6 5.3 %copy-start.3 = (f32[32,6144]{1,0:T(8,128)S(1)}, f32[32,6144]{1,0:T(8,128)}, u32[]{:S(2)}) copy-start(f32[32,6144]{1,0:T(8,128)} %mix.3) | copy-start | bytes 2359300
  5.9 7.9 %copy-start.12 = (f32[6144]{0:T(1024)S(1)}, f32[6144]{0:T(1024)}, u32[]{:S(2)}) copy-start(f32[6144]{0:T(1024)} %param.14) | copy-start | bytes 73732
  5.9 18.8 %copy-start.13 = (s32[1,48]{1,0:T(1,128)S(1)}, s32[1,48]{1,0:T(1,128)}, u32[]{:S(2)}) copy-start(s32[1,48]{1,0:T(1,128)} %param.17) | copy-start | bytes 580
  5.9 18.9 %copy-start.4 = (s32[12288,1]{0,1:T(1,128)S(1)}, s32[12288,1]{0,1:T(1,128)}, u32[]{:S(2)}) copy-start(s32[12288,1]{0,1:T(1,128)} %param.19) | copy-start | bytes 147460
  5.9 18.9 %copy-start.5 = (s32[12288]{0:T(1024)S(1)}, s32[12288]{0:T(1024)}, u32[]{:S(2)}) copy-start(s32[12288]{0:T(1024)} %param.18) | copy-start | bytes 147460
  5.9 18.9 %copy-start.6 = (f32[12288]{0:T(1024)S(1)}, f32[12288]{0:T(1024)}, u32[]{:S(2)}) copy-start(f32[12288]{0:T(1024)} %param.20) | copy-start | bytes 147460
  6.0 18.9 %copy-start.7 = (f32[12288]{0:T(1024)S(1)}, f32[12288]{0:T(1024)}, u32[]{:S(2)}) copy-start(f32[12288]{0:T(1024)} %param.21) | copy-start | bytes 147460
  8.7 2.7 %copy-start = (f32[32,6,6144]{2,1,0:T(8,128)}, f32[32,6,6144]{2,1,0:T(8,128)S(1)}, u32[]{:S(2)}) copy-start(f32[32,6,6144]{2,1,0:T(8,128)S(1)} %copy.18.air) | copy-start | bytes 14155780
  11.4 3.4 %collective-permute-start = (f32[7,6144]{1,0:T(8,128)S(1)}, f32[7,6144]{1,0:T(8,128)S(1)}, u32[]{:S(2)}, u32[]{:S(2)}) collective-permute-start(f32[7,6144]{1,0:T(8,128)S(1)} %shard_map.131), channel_id=1, source_target_pairs={{0,16},{1,17},{2,18},{3,19},{4,20},{5,21},{6,22},{7,23},{8,24},{9,... | collective-permute-start | bytes 516104 | tf_op jit(solution)/shard_map/ppermute | solution.py:354
  14.8 46.4 %copy-start.10 = (s32[15360]{0:T(1024)S(1)}, s32[15360]{0:T(1024)}, u32[]{:S(2)}) copy-start(s32[15360]{0:T(1024)} %param.22) | copy-start | bytes 184324
  14.8 46.5 %copy-start.11 = (f32[15360]{0:T(1024)S(1)}, f32[15360]{0:T(1024)}, u32[]{:S(2)}) copy-start(f32[15360]{0:T(1024)} %param.23) | copy-start | bytes 184324
  14.8 46.6 %copy-start.9 = (f32[6,3072]{1,0:T(8,128)S(1)}, f32[6,3072]{1,0:T(8,128)}, u32[]{:S(2)}) copy-start(f32[6,3072]{1,0:T(8,128)} %param.15) | copy-start | bytes 221188
  14.8 63.2 %copy-start.8 = (f32[3072]{0:T(1024)S(1)}, f32[3072]{0:T(1024)}, u32[]{:S(2)}) copy-start(f32[3072]{0:T(1024)} %param.16) | copy-start | bytes 36868
  20.8 2.7 %copy-start.1 = (f32[32,6,6144]{2,1,0:T(8,128)}, f32[32,6,6144]{2,1,0:T(8,128)S(1)}, u32[]{:S(2)}) copy-start(f32[32,6,6144]{2,1,0:T(8,128)S(1)} %get-tuple-element.9.parts) | copy-start | bytes 14155780
  23.4 23.4 %collective-permute-start.1 = (f32[2,7,6144]{2,1,0:T(8,128)S(1)}, f32[2,7,6144]{2,1,0:T(8,128)S(1)}, u32[]{:S(2)}, u32[]{:S(2)}) collective-permute-start(f32[2,7,6144]{2,1,0:T(8,128)S(1)} %get-tuple-element.11), channel_id=1, source_target_pairs={{16,0},{17,1},{18,2},{19,3},{20,4},{21,5},{22,6},{23,7},{24,8},{25... | collective-permute-start | bytes 1032200 | tf_op jit(solution)/shard_map/ppermute | solution.py:373
  53.7 24.3 %all-to-all-start = ((f32[128,8,128]{2,1,0:T(8,128)}), f32[128,8,128]{2,1,0:T(8,128)S(1)}, u32[]{:S(2)}, u32[]{:S(2)}) async-start(f32[128,8,128]{2,1,0:T(8,128)} %shard_map.134.sent), calls=%async_computation | async-start | bytes 1048576 | tf_op jit(solution)/shard_map/all_to_all | solution.py:383
  115.8 1.4 collective-permute-start.2
  178.4 1.4 collective-permute-start.3
  180.0 2.8 %copy-start.2 = (f32[32,6,6144]{2,1,0:T(8,128)S(1)}, f32[32,6,6144]{2,1,0:T(8,128)}, u32[]{:S(2)}) copy-start(f32[32,6,6144]{2,1,0:T(8,128)} %copy-done.1) | copy-start | bytes 14155780

commit v2 on v1

--- a/solution.py
+++ b/solution.py
@@ -22,10 +22,6 @@
 
 def pair(ref, i):
     return jnp.concatenate([ref[pl.ds(2 * i, 1), :], ref[pl.ds(2 * i + 1, 1), :]], axis=1)
-
-
-def wide(ref, i):
-    return jnp.concatenate([ref[2 * i], ref[2 * i + 1]], axis=1)
 
 
 def onehot(index, count):
@@ -121,7 +117,7 @@
         )
         return 0
 
-    lax.fori_loop(0, owner.shape[0] // 2, block, 0)
+    lax.fori_loop(0, owner.shape[0] // 2, block, 0, unroll=4)
     out[0] = acc[0:128]
     out[1] = acc[128:256]
     out[2] = acc[256:384] + acc[384:512]
@@ -240,91 +236,207 @@
     )(parts, ratios, below)
 
 
-def send_kernel(tracers, resid, slope, flux, other, block, column, gain, out):
-    rows = slope.shape[0]
-    flux_col = flux[...] + other[...]
-    bottom = resid[...] + jnp.concatenate([slope[...]] * tracers, axis=0) * flux_col
+def exchange_kernel(
+    tracers,
+    sections,
+    ring,
+    resid,
+    slope,
+    flux,
+    other,
+    block,
+    column,
+    flow,
+    coupling,
+    row,
+    lane,
+    sea,
+    rate,
+    flux_new,
+    sea_new,
+    sent,
+    arrived,
+    back,
+    returned,
+    acc,
+    out_send,
+    out_recv,
+    back_send,
+    back_recv,
+):
+    devices = sections * ring
+    rows, surf_rows = slope.shape[0], rate.shape[0]
+    parts = sent.shape[1] // tracers
+    me = lax.axis_index("sect") * ring + lax.axis_index("cols")
+
+    def coords(device):
+        return (device // ring, lax.rem(device, ring))
+
+    def ahead(s):
+        return lax.rem(me + s, devices)
+
+    def behind(s):
+        return lax.rem(me + devices - s, devices)
+
+    def outward(s):
+        device = ahead(s)
+        return pltpu.make_async_remote_copy(
+            src_ref=sent.at[device],
+            dst_ref=arrived.at[me],
+            send_sem=out_send.at[s],
+            recv_sem=out_recv.at[s],
+            device_id=coords(device),
+            device_id_type=pl.DeviceIdType.MESH,
+        )
+
+    def homeward(s):
+        device = ahead(s)
+        return pltpu.make_async_remote_copy(
+            src_ref=back.at[device],
+            dst_ref=returned.at[me],
+            send_sem=back_send.at[s],
+            recv_sem=back_recv.at[s],
+            device_id=coords(device),
+            device_id_type=pl.DeviceIdType.MESH,
+        )
+
+    def pack(values):
+        return jnp.concatenate(
+            [values[:, p * LANES : (p + 1) * LANES] for p in range(parts)], axis=0
+        )
+
+    def unpack(values):
+        return jnp.concatenate(
+            [values[p * tracers : (p + 1) * tracers] for p in range(parts)], axis=1
+        )
+
+    barrier = pltpu.get_barrier_semaphore()
+
+    def greet(s, _):
+        pl.semaphore_signal(
+            barrier,
+            inc=1,
+            device_id=coords(ahead(s)),
+            device_id_type=pl.DeviceIdType.MESH,
+        )
+        return 0
+
+    lax.fori_loop(1, devices, greet, 0)
+    bottom = resid[...] + jnp.concatenate([slope[...]] * tracers, axis=0) * (flux[...] + other[...])
     table = table_of(bottom)
 
-    def step(i, _):
-        at = gather_step(table, pair(block, i), pair(column, i), rows, tracers)
-        sent = jnp.concatenate(
-            [at, pair(gain, i), jnp.zeros((7 - tracers, 2 * LANES), jnp.float32)], axis=0
-        )
-        out[2 * i] = sent[:, 0:LANES]
-        out[2 * i + 1] = sent[:, LANES:]
-        return 0
-
-    lax.fori_loop(0, block.shape[0] // 2, step, 0, unroll=4)
-
-
-def send(tracers, resid, slope, flux, other, block, column, gain):
+    def at_cells(device):
+        here = pl.ds(device, 1)
+        return pack(gather_step(table, block[here, :], column[here, :], rows, tracers))
+
+    own = at_cells(me)
+    sent[me] = own
+    pl.semaphore_wait(barrier, devices - 1)
+
+    def send(s, _):
+        device = ahead(s)
+        sent[device] = at_cells(device)
+        outward(s).start()
+        return 0
+
+    lax.fori_loop(1, devices, send, 0)
+    acc[...] = jnp.zeros_like(acc)
+
+    def add(values, device):
+        here = pl.ds(device, 1)
+        strength = coupling[here, :]
+        scatter_step(
+            acc,
+            jnp.concatenate([unpack(values) * strength, strength], axis=0),
+            row[here, :],
+            lane[here, :],
+            surf_rows,
+        )
+
+    add(own, me)
+
+    def receive(s, _):
+        outward(s).wait_recv()
+        device = behind(s)
+        add(arrived[device], device)
+        return 0
+
+    lax.fori_loop(1, devices, receive, 0)
+    pace = rate[...]
+    inverse = 1.0 / (1.0 + pace * acc[tracers * surf_rows : (tracers + 1) * surf_rows])
+    for q in range(tracers):
+        here = slice(q * surf_rows, (q + 1) * surf_rows)
+        sea_new[here] = (sea[here] + pace * acc[here]) * inverse
+    sea_table = table_of(sea_new[...])
+
+    def seen(device):
+        here = pl.ds(device, 1)
+        return pack(gather_step(sea_table, row[here, :], lane[here, :], surf_rows, tracers))
+
+    def give_back(s, _):
+        device = ahead(s)
+        back[device] = seen(device)
+        homeward(s).start()
+        return 0
+
+    lax.fori_loop(1, devices, give_back, 0)
+    flux_new[...] = jnp.zeros_like(flux_new)
+
+    def collect(values, device):
+        here = pl.ds(device, 1)
+        scatter_step(
+            flux_new,
+            unpack(values - sent[device]) * flow[here, :],
+            block[here, :],
+            column[here, :],
+            rows,
+        )
+
+    collect(seen(me), me)
+
+    def take_back(s, _):
+        homeward(s).wait_recv()
+        device = behind(s)
+        collect(returned[device], device)
+        return 0
+
+    lax.fori_loop(1, devices, take_back, 0)
+
+    def finish(s, _):
+        outward(s).wait_send()
+        homeward(s).wait_send()
+        return 0
+
+    lax.fori_loop(1, devices, finish, 0)
+
+
+def exchange(tracers, sections, ring, resid, slope, flux, other, block, column, flow, *surface):
+    devices, slots = block.shape
+    surf_rows = surface[-1].shape[0]
+    landing = pltpu.VMEM((devices, tracers * slots // LANES, LANES), jnp.float32)
     return pl.pallas_call(
-        functools.partial(send_kernel, tracers),
-        out_shape=jax.ShapeDtypeStruct((block.shape[0], 8, LANES), jnp.float32),
-        compiler_params=PARAMS,
-    )(resid, slope, flux, other, block, column, gain)
-
-
-def surface_kernel(tracers, arrived, frac, row, lane, sea, rate, out, sea_new, acc):
-    rows = rate.shape[0]
-    acc[...] = jnp.zeros_like(acc)
-
-    def gathering(i, _):
-        came = wide(arrived, i)
-        coupling = came[tracers : tracers + 1] * pair(frac, i)
-        values = jnp.concatenate([came[0:tracers] * coupling, coupling], axis=0)
-        scatter_step(acc, values, pair(row, i), pair(lane, i), rows)
-        return 0
-
-    lax.fori_loop(0, row.shape[0] // 2, gathering, 0, unroll=4)
-    strength = rate[...]
-    inverse = 1.0 / (1.0 + strength * acc[tracers * rows : (tracers + 1) * rows])
-    for q in range(tracers):
-        here = slice(q * rows, (q + 1) * rows)
-        sea_new[here] = (sea[here] + strength * acc[here]) * inverse
-    table = table_of(sea_new[...])
-
-    def returning(i, _):
-        seen = gather_step(table, pair(row, i), pair(lane, i), rows, tracers)
-        sent = jnp.concatenate([seen, jnp.zeros((8 - tracers, 2 * LANES), jnp.float32)], axis=0)
-        out[2 * i] = sent[:, 0:LANES]
-        out[2 * i + 1] = sent[:, LANES:]
-        return 0
-
-    lax.fori_loop(0, row.shape[0] // 2, returning, 0, unroll=4)
-
-
-def surface(tracers, arrived, frac, row, lane, sea, rate):
-    return pl.pallas_call(
-        functools.partial(surface_kernel, tracers),
+        functools.partial(exchange_kernel, tracers, sections, ring),
         out_shape=[
-            jax.ShapeDtypeStruct(arrived.shape, jnp.float32),
-            jax.ShapeDtypeStruct(sea.shape, jnp.float32),
-        ],
-        scratch_shapes=[pltpu.VMEM(((tracers + 1) * rate.shape[0], LANES), jnp.float32)],
-        compiler_params=PARAMS,
-    )(arrived, frac, row, lane, sea, rate)
-
-
-def collect_kernel(tracers, returned, sent, flow, block, column, flux):
-    rows = flux.shape[0] // tracers
-    flux[...] = jnp.zeros_like(flux)
-
-    def step(i, _):
-        values = (wide(returned, i) - wide(sent, i))[0:tracers] * pair(flow, i)
-        scatter_step(flux, values, pair(block, i), pair(column, i), rows)
-        return 0
-
-    lax.fori_loop(0, block.shape[0] // 2, step, 0, unroll=4)
-
-
-def collect(tracers, rows, returned, sent, flow, block, column):
-    return pl.pallas_call(
-        functools.partial(collect_kernel, tracers),
-        out_shape=jax.ShapeDtypeStruct((tracers * rows, LANES), jnp.float32),
-        compiler_params=PARAMS,
-    )(returned, sent, flow, block, column)
+            jax.ShapeDtypeStruct(resid.shape, jnp.float32),
+            jax.ShapeDtypeStruct((tracers * surf_rows, LANES), jnp.float32),
+        ],
+        in_specs=[pl.BlockSpec(memory_space=pltpu.VMEM)] * 12,
+        out_specs=[pl.BlockSpec(memory_space=pltpu.VMEM)] * 2,
+        scratch_shapes=[
+            landing,
+            landing,
+            landing,
+            landing,
+            pltpu.VMEM(((tracers + 1) * surf_rows, LANES), jnp.float32),
+            pltpu.SemaphoreType.DMA((devices,)),
+            pltpu.SemaphoreType.DMA((devices,)),
+            pltpu.SemaphoreType.DMA((devices,)),
+            pltpu.SemaphoreType.DMA((devices,)),
+        ],
+        compiler_params=pltpu.CompilerParams(
+            vmem_limit_bytes=40 * 1024 * 1024, collective_id=0, has_side_effects=True
+        ),
+    )(resid, slope, flux, other, block, column, flow, *surface)
 
 
 def body(
@@ -361,11 +473,13 @@
         devices,
         cap_rows,
     )
+    slots = slots.reshape(4, LANES * LANES)[:, : devices * cap_rows * LANES]
+    slots = slots.reshape(4, devices, cap_rows * LANES)
     block = slots[0].astype(jnp.int32)
     column = slots[1].astype(jnp.int32)
-    gain, flow = slots[2], slots[3]
-    cell = jnp.pad(slot_cell.reshape(devices, capacity), padding).reshape(-1, LANES)
-    frac = jnp.pad(slot_frac.reshape(devices, capacity), padding).reshape(-1, LANES)
+    gain = lax.all_to_all(slots[2], ("sect", "cols"), split_axis=0, concat_axis=0, tiled=True)
+    cell = jnp.pad(slot_cell.reshape(devices, capacity), padding)
+    coupling = gain * jnp.pad(slot_frac.reshape(devices, capacity), padding)
     row, lane = cell // LANES, cell % LANES
 
     last = jnp.where(is_lower, flux_scale, mix_coef[-1])[None]
@@ -379,11 +493,23 @@
     rate = sea_rate.reshape(surf_rows, LANES)
     flux = other = jnp.zeros((tracers * rows, LANES), jnp.float32)
     for _ in range(SUBSTEPS):
-        sent = send(tracers, resid, slope, flux, other, block, column, gain)
-        arrived = lax.all_to_all(sent, ("sect", "cols"), split_axis=0, concat_axis=0, tiled=True)
-        back, sea = surface(tracers, arrived, frac, row, lane, sea, rate)
-        returned = lax.all_to_all(back, ("sect", "cols"), split_axis=0, concat_axis=0, tiled=True)
-        flux = collect(tracers, rows, returned, sent, flow, block, column)
+        flux, sea = exchange(
+            tracers,
+            lax.axis_size("sect"),
+            lax.axis_size("cols"),
+            resid,
+            slope,
+            flux,
+            other,
+            block,
+            column,
+            slots[3],
+            coupling,
+            row,
+            lane,
+            sea,
+            rate,
+        )
         other = lax.ppermute(flux, "sect", [(0, 1), (1, 0)])
     flux_col = (flux + other).reshape(tracers, columns)
     below = jnp.where(is_lower, flux_col, low[1, :tracers] + low[1, tracers] * flux_col)

time: 190 us -> 143 us (0.75)
  blocking collectives: 55.7 us -> 0 us
  Pallas kernels: 82.6 us -> 106 us
  waiting for transfers between devices: 19.5 us -> 3.8 us
    all_to_all x3 -> x0, blocking collectives: 55.7 us -> none  [the longest x2 37.1 us: body(): lax.all_to_all(back, ('sect', 'cols'), split_axis=0, concat_axis=0, tiled...]
    pallas_call x6 -> x2, Pallas kernels: 50 us -> 78.3 us  [exchange(): pl.pallas_call(functools.partial(exchange_kernel, tracers, sections, ring...]
    all_to_all x1, waiting for transfers between devices: 16.5 us -> 0.01 us  [body(): lax.all_to_all(slots[2], ('sect', 'cols'), split_axis=0, concat_axis=0, t...]
    pallas_call x1, Pallas kernels: 22 us -> 17.5 us  [setup(): pl.pallas_call(functools.partial(setup_kernel, devices, cap_rows), out_sh...]
  transfers between devices with their start and end apart: 5 -> 5, of which waited for: 4 -> 3; matrix products, arithmetic and copies ran while one was open for 1% -> 1% of each run, Pallas kernels for 12% -> 16%
where the time goes in v2:
time: 143 us; the launch traced here: 142 us
  Pallas kernels  106 us (74%)
  local copies, waits for them, and re-layouts  19.4 us (14%)
  starting transfers between devices  10.8 us (8%)
  waiting for transfers between devices  3.8 us (3%)
    pallas_call x2, Pallas kernels, exchange(): pl.pallas_call(functools.partial(exchange_kernel, tracers, sections, ring...  78.3 us
    unnamed x30, local copies, waits for them, and re-layouts  18.3 us
    pallas_call x1, Pallas kernels, setup(): pl.pallas_call(functools.partial(setup_kernel, devices, cap_rows), out_sh...  17.5 us
    all_to_all x1, starting transfers between devices, body(): lax.all_to_all(slots[2], ('sect', 'cols'), split_axis=0, concat_axis=0, t...  6.68 us
    pallas_call x1, Pallas kernels, descend(): pl.pallas_call(descend_kernel, grid=(columns // COL_TILE,), in_specs=[pl....  5.95 us
  transfers between devices with their start and end apart: 5, of which 3 were waited for; matrix products, arithmetic and copies ran while one was open for 1% of the time, Pallas kernels for 16%

profile of v2, /device:TPU:0, one launch (start us, length us, event | category | flops | bytes accessed | tf_op | source)
XLA Modules:
  0.0 142.3 jit_solution(10954281098825874246)
XLA Ops:
  0.6 0.0 copy-start.3
  0.6 5.2 %copy.21.air = f32[32,6,6144]{2,1,0:T(8,128)S(1)} copy(f32[32,6,6144]{2,0,1:T(8,128)} %param.12) | data formatting | bytes 9437184 | tf_op args[0]
  5.9 0.0 copy-done.3
  5.9 0.0 copy-start.13
  5.9 0.0 copy-start.4
  5.9 0.0 copy-start.5
  5.9 0.0 copy-start.6
  5.9 0.0 copy-start.7
  6.0 0.0 copy-start.12
  6.0 0.0 copy-start.10
  6.0 2.7 %shard_map.131 = f32[7,6144]{1,0:T(8,128)S(1)} custom-call(f32[32,6,6144]{2,1,0:T(8,128)S(1)} %copy.21.air, f32[32,6144]{1,0:T(8,128)S(1)} %copy-done.3), custom_call_target="tpu_custom_call" | custom-call | tf_op jit(solution)/shard_map/pallas_call | solution.py:157
  8.7 0.0 copy-start
  8.7 2.6 %copy-done = f32[32,6,6144]{2,1,0:T(8,128)} copy-done((f32[32,6,6144]{2,1,0:T(8,128)}, f32[32,6,6144]{2,1,0:T(8,128)S(1)}, u32[]{:S(2)}) %copy-start) | copy-done | bytes 4718616
  11.4 0.0 copy-start.11
  11.4 0.0 copy-start.9
  11.4 0.0 copy-start.8
  11.4 2.5 %collective-permute-start = (f32[7,6144]{1,0:T(8,128)S(1)}, f32[7,6144]{1,0:T(8,128)S(1)}, u32[]{:S(2)}, u32[]{:S(2)}) collective-permute-start(f32[7,6144]{1,0:T(8,128)S(1)} %shard_map.131), channel_id=1, source_target_pairs={{0,16},{1,17},{2,18},{3,19},{4,20},{5,21},{6,22},{7,23},{8,24},{9,... | collective-permute-start | bytes 516104 | tf_op jit(solution)/shard_map/ppermute | solution.py:466
  13.9 0.0 copy-done.13
  13.9 0.1 broadcast_in_dim.16.counts
  14.0 0.0 copy-done.4
  14.0 0.0 copy-done.5
  14.0 0.0 copy-done.6
  14.0 0.0 copy-done.7
  14.0 17.5 %shard_map.133 = f32[4,128,128]{2,1,0:T(8,128)S(1)} custom-call(s32[96,128]{1,0:T(8,128)S(1)} %bitcast.22, s32[96,128]{1,0:T(8,128)S(1)} %bitcast.23, f32[96,128]{1,0:T(8,128)S(1)} %bitcast.24, f32[96,128]{1,0:T(8,128)S(1)} %bitcast.25, s32[48,128]{1,0:T(8,128)S(1)} %broadcast_in_dim.16.counts), custom_call_target="tpu_custom_call" | custom-call | tf_op jit(solution)/shard_map/pallas_call | solution.py:128
  31.5 0.6 fusion.5
  32.1 6.7 %all-to-all-start = ((f32[32,1,512]{2,1,0:T(1,128)}), f32[32,1,512]{2,1,0:T(1,128)S(1)}, u32[]{:S(2)}, u32[]{:S(2)}) async-start(f32[32,1,512]{2,1,0:T(1,128)} %bitcast.8), calls=%async_computation | async-start | bytes 131072 | tf_op jit(solution)/shard_map/all_to_all | solution.py:480
  38.8 0.0 copy-done.12
  38.9 0.0 collective-permute-done.start
  38.9 5.9 %shard_map.132 = (f32[32,6,6144]{2,1,0:T(8,128)S(1)}, f32[32,6144]{1,0:T(8,128)S(1)}, f32[2,7,6144]{2,1,0:T(8,128)S(1)}) custom-call(f32[32,6,6144]{2,1,0:T(8,128)} %copy-done, f32[32,6144]{1,0:T(8,128)S(1)} %copy-done.3, f32[7,6144]{1,0:T(8,128)S(1)} %collective-permute-done.start, f32[1,6144]{1,0:T(1,128)S(1)} %bitcast.21), custom_call_target="tpu_custom_call" | custom-call | tf_op jit(solution)/shard_map/pallas_call | solution.py:193
  44.8 0.0 copy-start.1
  44.8 2.6 %copy-done.1 = f32[32,6,6144]{2,1,0:T(8,128)} copy-done((f32[32,6,6144]{2,1,0:T(8,128)}, f32[32,6,6144]{2,1,0:T(8,128)S(1)}, u32[]{:S(2)}) %copy-start.1) | copy-done | bytes 4718616
  47.5 1.5 %collective-permute-start.1 = (f32[2,7,6144]{2,1,0:T(8,128)S(1)}, f32[2,7,6144]{2,1,0:T(8,128)S(1)}, u32[]{:S(2)}, u32[]{:S(2)}) collective-permute-start(f32[2,7,6144]{2,1,0:T(8,128)S(1)} %get-tuple-element.11), channel_id=1, source_target_pairs={{16,0},{17,1},{18,2},{19,3},{20,4},{21,5},{22,6},{23,7},{24,8},{25... | collective-permute-start | bytes 1032200 | tf_op jit(solution)/shard_map/ppermute | solution.py:487
  49.0 0.0 copy-done.10
  49.0 0.1 reshape.54
  49.1 0.0 copy-done.11
  49.1 0.1 reshape.55
  49.2 0.0 copy-done.9
  49.3 0.1 add_select_fusion
  49.3 0.0 all-to-all-done
  49.4 1.7 %collective-permute-done.1 = f32[2,7,6144]{2,1,0:T(8,128)S(1)} collective-permute-done((f32[2,7,6144]{2,1,0:T(8,128)S(1)}, f32[2,7,6144]{2,1,0:T(8,128)S(1)}, u32[]{:S(2)}, u32[]{:S(2)}) %collective-permute-start.1) | collective-permute-done | bytes 344096 | tf_op jit(solution)/shard_map/ppermute | solution.py:487
  51.1 0.1 broadcast_select_fusion
  51.2 0.1 fusion.4
  51.3 0.0 copy-done.8
  51.3 41.4 %shard_map.134 = (f32[288,128]{1,0:T(8,128)S(1)}, f32[144,128]{1,0:T(8,128)S(1)}) custom-call(f32[288,128]{1,0:T(8,128)S(1)} %reshape_squeeze.6.resid, f32[48,128]{1,0:T(8,128)S(1)} %bitcast.19, f32[288,128]{1,0:T(8,128)S(1)} %broadcast_in_dim.14.flux.other, f32[288,128]{1,0:T(8,128)S(1)} %broadcast_in_dim.14.flux.other, ...), custom_call_target="tpu_custom_call" | custom-call | tf_op jit(solution)/shard_map/pallas_call | solution.py:417
  92.8 0.1 collective-permute-start.2
  92.9 1.4 collective-permute-done.2.other
  94.2 36.8 %shard_map.135 = (f32[288,128]{1,0:T(8,128)S(1)}, f32[144,128]{1,0:T(8,128)S(1)}) custom-call(f32[288,128]{1,0:T(8,128)S(1)} %reshape_squeeze.6.resid, f32[48,128]{1,0:T(8,128)S(1)} %bitcast.20, f32[288,128]{1,0:T(8,128)S(1)} %get-tuple-element.12.flux, f32[288,128]{1,0:T(8,128)S(1)} %collective-permute-done.2.other, ...), custom_call_target="tpu_custom_call" | custom-call | tf_op jit(solution)/shard_map/pallas_call | solution.py:417
  131.1 0.1 collective-permute-start.3
  131.1 0.7 reshape.59
  131.8 0.7 collective-permute-done.3
  132.6 0.0 copy-start.2
  132.6 2.8 %copy-done.2 = f32[32,6,6144]{2,1,0:T(8,128)S(1)} copy-done((f32[32,6,6144]{2,1,0:T(8,128)S(1)}, f32[32,6,6144]{2,1,0:T(8,128)}, u32[]{:S(2)}) %copy-start.2) | copy-done | bytes 4718616
  135.4 1.9 %shard_map.136 = f32[32,6,6144]{2,1,0:T(8,128)S(1)} custom-call(f32[32,6,6144]{2,1,0:T(8,128)S(1)} %copy-done.2, f32[32,6144]{1,0:T(8,128)S(1)} %get-tuple-element.10.ratios, f32[6,6144]{1,0:T(8,128)S(1)} %fusion.1.below), custom_call_target="tpu_custom_call" | custom-call | tf_op jit(solution)/shard_map/pallas_call | solution.py:225
  137.3 4.9 %copy.23 = f32[32,6,6144]{2,0,1:T(8,128)} copy(f32[32,6,6144]{2,1,0:T(8,128)S(1)} %shard_map.136) | data formatting | bytes 9437184
  (13 shorter events, 0.3 us)
Async XLA Ops:
  0.6 5.3 %copy-start.3 = (f32[32,6144]{1,0:T(8,128)S(1)}, f32[32,6144]{1,0:T(8,128)}, u32[]{:S(2)}) copy-start(f32[32,6144]{1,0:T(8,128)} %mix.3) | copy-start | bytes 2359300
  5.9 8.0 %copy-start.13 = (s32[1,48]{1,0:T(1,128)S(1)}, s32[1,48]{1,0:T(1,128)}, u32[]{:S(2)}) copy-start(s32[1,48]{1,0:T(1,128)} %param.17) | copy-start | bytes 580
  5.9 8.1 %copy-start.4 = (s32[12288,1]{0,1:T(1,128)S(1)}, s32[12288,1]{0,1:T(1,128)}, u32[]{:S(2)}) copy-start(s32[12288,1]{0,1:T(1,128)} %param.19) | copy-start | bytes 147460
  5.9 8.1 %copy-start.5 = (s32[12288]{0:T(1024)S(1)}, s32[12288]{0:T(1024)}, u32[]{:S(2)}) copy-start(s32[12288]{0:T(1024)} %param.18) | copy-start | bytes 147460
  5.9 8.0 %copy-start.6 = (f32[12288]{0:T(1024)S(1)}, f32[12288]{0:T(1024)}, u32[]{:S(2)}) copy-start(f32[12288]{0:T(1024)} %param.20) | copy-start | bytes 147460
  5.9 8.0 %copy-start.7 = (f32[12288]{0:T(1024)S(1)}, f32[12288]{0:T(1024)}, u32[]{:S(2)}) copy-start(f32[12288]{0:T(1024)} %param.21) | copy-start | bytes 147460
  6.0 32.9 %copy-start.12 = (f32[6144]{0:T(1024)S(1)}, f32[6144]{0:T(1024)}, u32[]{:S(2)}) copy-start(f32[6144]{0:T(1024)} %param.14) | copy-start | bytes 73732
  6.0 43.0 %copy-start.10 = (f32[15360]{0:T(1024)S(1)}, f32[15360]{0:T(1024)}, u32[]{:S(2)}) copy-start(f32[15360]{0:T(1024)} %param.23) | copy-start | bytes 184324
  8.7 2.7 %copy-start = (f32[32,6,6144]{2,1,0:T(8,128)}, f32[32,6,6144]{2,1,0:T(8,128)S(1)}, u32[]{:S(2)}) copy-start(f32[32,6,6144]{2,1,0:T(8,128)S(1)} %copy.21.air) | copy-start | bytes 14155780
  11.4 37.7 %copy-start.11 = (s32[15360]{0:T(1024)S(1)}, s32[15360]{0:T(1024)}, u32[]{:S(2)}) copy-start(s32[15360]{0:T(1024)} %param.22) | copy-start | bytes 184324
  11.4 37.8 %copy-start.9 = (f32[6,3072]{1,0:T(8,128)S(1)}, f32[6,3072]{1,0:T(8,128)}, u32[]{:S(2)}) copy-start(f32[6,3072]{1,0:T(8,128)} %param.15) | copy-start | bytes 221188
  11.4 39.9 %copy-start.8 = (f32[3072]{0:T(1024)S(1)}, f32[3072]{0:T(1024)}, u32[]{:S(2)}) copy-start(f32[3072]{0:T(1024)} %param.16) | copy-start | bytes 36868
  11.4 27.5 %collective-permute-start = (f32[7,6144]{1,0:T(8,128)S(1)}, f32[7,6144]{1,0:T(8,128)S(1)}, u32[]{:S(2)}, u32[]{:S(2)}) collective-permute-start(f32[7,6144]{1,0:T(8,128)S(1)} %shard_map.131), channel_id=1, source_target_pairs={{0,16},{1,17},{2,18},{3,19},{4,20},{5,21},{6,22},{7,23},{8,24},{9,... | collective-permute-start | bytes 516104 | tf_op jit(solution)/shard_map/ppermute | solution.py:466
  32.1 17.2 %all-to-all-start = ((f32[32,1,512]{2,1,0:T(1,128)}), f32[32,1,512]{2,1,0:T(1,128)S(1)}, u32[]{:S(2)}, u32[]{:S(2)}) async-start(f32[32,1,512]{2,1,0:T(1,128)} %bitcast.8), calls=%async_computation | async-start | bytes 131072 | tf_op jit(solution)/shard_map/all_to_all | solution.py:480
  44.8 2.7 %copy-start.1 = (f32[32,6,6144]{2,1,0:T(8,128)}, f32[32,6,6144]{2,1,0:T(8,128)S(1)}, u32[]{:S(2)}) copy-start(f32[32,6,6144]{2,1,0:T(8,128)S(1)} %get-tuple-element.9.parts) | copy-start | bytes 14155780
  47.5 3.6 %collective-permute-start.1 = (f32[2,7,6144]{2,1,0:T(8,128)S(1)}, f32[2,7,6144]{2,1,0:T(8,128)S(1)}, u32[]{:S(2)}, u32[]{:S(2)}) collective-permute-start(f32[2,7,6144]{2,1,0:T(8,128)S(1)} %get-tuple-element.11), channel_id=1, source_target_pairs={{16,0},{17,1},{18,2},{19,3},{20,4},{21,5},{22,6},{23,7},{24,8},{25... | collective-permute-start | bytes 1032200 | tf_op jit(solution)/shard_map/ppermute | solution.py:487
  92.8 1.4 %collective-permute-start.2 = (f32[288,128]{1,0:T(8,128)S(1)}, f32[288,128]{1,0:T(8,128)S(1)}, u32[]{:S(2)}, u32[]{:S(2)}) collective-permute-start(f32[288,128]{1,0:T(8,128)S(1)} %get-tuple-element.12.flux), channel_id=1, source_target_pairs={{0,16},{16,0},{1,17},{17,1},{2,18},{18,2},{3,19},{19,3},{4,20},{20... | collective-permute-start | bytes 442376 | tf_op jit(solution)/shard_map/ppermute | solution.py:513
  131.1 1.4 %collective-permute-start.3 = (f32[288,128]{1,0:T(8,128)S(1)}, f32[288,128]{1,0:T(8,128)S(1)}, u32[]{:S(2)}, u32[]{:S(2)}) collective-permute-start(f32[288,128]{1,0:T(8,128)S(1)} %get-tuple-element.14), channel_id=1, source_target_pairs={{0,16},{16,0},{1,17},{17,1},{2,18},{18,2},{3,19},{19,3},{4,20},{20... | collective-permute-start | bytes 442376 | tf_op jit(solution)/shard_map/ppermute | solution.py:513
  132.6 2.8 %copy-start.2 = (f32[32,6,6144]{2,1,0:T(8,128)S(1)}, f32[32,6,6144]{2,1,0:T(8,128)}, u32[]{:S(2)}) copy-start(f32[32,6,6144]{2,1,0:T(8,128)} %copy-done.1) | copy-start | bytes 14155780

commit v3 on v2

--- a/solution.py
+++ b/solution.py
@@ -32,18 +32,21 @@
     return jnp.where(onehot(lane, LANES), 1.0, 0.0).astype(jnp.bfloat16)
 
 
+def spread(mask, values):
+    values = values.astype(jnp.bfloat16)
+    return jnp.concatenate([mask * values[q : q + 1] for q in range(values.shape[0])], axis=0)
+
+
+def one_hot(index, count):
+    return jnp.where(onehot(index, count), 1.0, 0.0).astype(jnp.bfloat16)
+
+
 def scatter_step(acc, values, row, lane, rows):
-    mask = onehot(row, rows)
+    mask = one_hot(row, rows)
     high, low = split(values)
-    left = [
-        jnp.concatenate(
-            [jnp.where(mask, part[q : q + 1], 0.0) for q in range(values.shape[0])], axis=0
-        ).astype(jnp.bfloat16)
-        for part in (high, low)
-    ]
     lane_hot = lanes_map(lane)
     acc[...] += lax.dot_general(
-        jnp.concatenate(left, axis=1),
+        jnp.concatenate([spread(mask, high), spread(mask, low)], axis=1),
         jnp.concatenate([lane_hot, lane_hot], axis=1),
         (((1,), (1,)), ((), ())),
         preferred_element_type=jnp.float32,
@@ -105,12 +108,8 @@
             ],
             axis=0,
         )
-        mask = onehot(own * cap_rows + rank // LANES, LANES)
-        left = jnp.concatenate(
-            [jnp.where(mask, values[q : q + 1], 0.0) for q in range(6)], axis=0
-        ).astype(jnp.bfloat16)
         acc[...] += lax.dot_general(
-            left,
+            spread(one_hot(own * cap_rows + rank // LANES, LANES), values),
             lanes_map(rank % LANES),
             (((1,), (1,)), ((), ())),
             preferred_element_type=jnp.float32,
@@ -146,19 +145,20 @@
 
 def descend_end_kernel(air, mix, end):
     under = jnp.zeros((1, end.shape[1]), jnp.float32)
-    carried = jnp.zeros((air.shape[1], end.shape[1]), jnp.float32)
-    for k in range(air.shape[0]):
-        _, _, _, under, carried = level_down(mix, air, k, under, carried)
+    carried = jnp.zeros((air.shape[0], end.shape[1]), jnp.float32)
+    levels_first = jnp.swapaxes(air[...], 0, 1)
+    for k in range(air.shape[1]):
+        _, _, _, under, carried = level_down(mix, levels_first, k, under, carried)
     end[...] = jnp.concatenate([carried, under], axis=0)
 
 
 def descend_end(air, mix):
-    levels, tracers, columns = air.shape
+    tracers, levels, columns = air.shape
     return pl.pallas_call(
         descend_end_kernel,
         grid=(columns // COL_TILE,),
         in_specs=[
-            pl.BlockSpec((levels, tracers, COL_TILE), lambda j: (0, 0, j)),
+            pl.BlockSpec((tracers, levels, COL_TILE), lambda j: (0, 0, j)),
             pl.BlockSpec((levels, COL_TILE), lambda j: (0, j)),
         ],
         out_specs=pl.BlockSpec((tracers + 1, COL_TILE), lambda j: (0, j)),
@@ -168,11 +168,12 @@
 
 
 def descend_kernel(air, mix, start, last, parts, ratios, ends):
-    levels, tracers, _ = air.shape
+    tracers, levels, _ = air.shape
+    levels_first = jnp.swapaxes(air[...], 0, 1)
     carried = start[0:tracers, :]
     under = start[tracers : tracers + 1, :]
     for k in range(levels):
-        part, ratio, inverse, under, carried = level_down(mix, air, k, under, carried)
+        part, ratio, inverse, under, carried = level_down(mix, levels_first, k, under, carried)
         parts[k] = part
         if k == levels - 1:
             ratio = last[...] * inverse
@@ -189,12 +190,12 @@
 
 
 def descend(air, mix, start, last):
-    levels, tracers, columns = air.shape
+    tracers, levels, columns = air.shape
     return pl.pallas_call(
         descend_kernel,
         grid=(columns // COL_TILE,),
         in_specs=[
-            pl.BlockSpec((levels, tracers, COL_TILE), lambda j: (0, 0, j)),
+            pl.BlockSpec((tracers, levels, COL_TILE), lambda j: (0, 0, j)),
             pl.BlockSpec((levels, COL_TILE), lambda j: (0, j)),
             pl.BlockSpec((tracers + 1, COL_TILE), lambda j: (0, j)),
             pl.BlockSpec((1, COL_TILE), lambda j: (0, j)),
@@ -205,7 +206,7 @@
             pl.BlockSpec((2, tracers + 1, COL_TILE), lambda j: (0, 0, j)),
         ],
         out_shape=[
-            jax.ShapeDtypeStruct(air.shape, jnp.float32),
+            jax.ShapeDtypeStruct((levels, tracers, columns), jnp.float32),
             jax.ShapeDtypeStruct(mix.shape, jnp.float32),
             jax.ShapeDtypeStruct((2, tracers + 1, columns), jnp.float32),
         ],
@@ -215,9 +216,11 @@
 
 def ascend_kernel(parts, ratios, below, out):
     value = below[...]
+    risen = []
     for k in range(parts.shape[0] - 1, -1, -1):
         value = parts[k] + ratios[k : k + 1, :] * value
-        out[k] = value
+        risen.append(value)
+    out[...] = jnp.swapaxes(jnp.stack(risen[::-1]), 0, 1)
 
 
 def ascend(parts, ratios, below):
@@ -230,8 +233,8 @@
             pl.BlockSpec((levels, COL_TILE), lambda j: (0, j)),
             pl.BlockSpec((tracers, COL_TILE), lambda j: (0, j)),
         ],
-        out_specs=pl.BlockSpec((levels, tracers, COL_TILE), lambda j: (0, 0, j)),
-        out_shape=jax.ShapeDtypeStruct(parts.shape, jnp.float32),
+        out_specs=pl.BlockSpec((tracers, levels, COL_TILE), lambda j: (0, 0, j)),
+        out_shape=jax.ShapeDtypeStruct((tracers, levels, columns), jnp.float32),
         compiler_params=PARAMS,
     )(parts, ratios, below)
 
@@ -247,7 +250,8 @@
     block,
     column,
     flow,
-    coupling,
+    gain,
+    frac,
     row,
     lane,
     sea,
@@ -266,7 +270,8 @@
 ):
     devices = sections * ring
     rows, surf_rows = slope.shape[0], rate.shape[0]
-    parts = sent.shape[1] // tracers
+    parts = back.shape[1] // tracers
+    acc_rows = acc.shape[0] // (tracers + 1)
     me = lax.axis_index("sect") * ring + lax.axis_index("cols")
 
     def coords(device):
@@ -306,9 +311,8 @@
         )
 
     def unpack(values):
-        return jnp.concatenate(
-            [values[p * tracers : (p + 1) * tracers] for p in range(parts)], axis=1
-        )
+        count = values.shape[0] // parts
+        return jnp.concatenate([values[p * count : (p + 1) * count] for p in range(parts)], axis=1)
 
     barrier = pltpu.get_barrier_semaphore()
 
@@ -327,7 +331,8 @@
 
     def at_cells(device):
         here = pl.ds(device, 1)
-        return pack(gather_step(table, block[here, :], column[here, :], rows, tracers))
+        picked = gather_step(table, block[here, :], column[here, :], rows, tracers)
+        return pack(jnp.concatenate([picked, gain[here, :]], axis=0))
 
     own = at_cells(me)
     sent[me] = own
@@ -344,13 +349,14 @@
 
     def add(values, device):
         here = pl.ds(device, 1)
-        strength = coupling[here, :]
+        came = unpack(values)
+        strength = came[tracers:] * frac[here, :]
         scatter_step(
             acc,
-            jnp.concatenate([unpack(values) * strength, strength], axis=0),
+            jnp.concatenate([came[0:tracers] * strength, strength], axis=0),
             row[here, :],
             lane[here, :],
-            surf_rows,
+            acc_rows,
         )
 
     add(own, me)
@@ -363,10 +369,11 @@
 
     lax.fori_loop(1, devices, receive, 0)
     pace = rate[...]
-    inverse = 1.0 / (1.0 + pace * acc[tracers * surf_rows : (tracers + 1) * surf_rows])
+    inverse = 1.0 / (1.0 + pace * acc[tracers * acc_rows : tracers * acc_rows + surf_rows])
     for q in range(tracers):
         here = slice(q * surf_rows, (q + 1) * surf_rows)
-        sea_new[here] = (sea[here] + pace * acc[here]) * inverse
+        summed = acc[q * acc_rows : q * acc_rows + surf_rows]
+        sea_new[here] = (sea[here] + pace * summed) * inverse
     sea_table = table_of(sea_new[...])
 
     def seen(device):
@@ -386,7 +393,7 @@
         here = pl.ds(device, 1)
         scatter_step(
             flux_new,
-            unpack(values - sent[device]) * flow[here, :],
+            (unpack(values) - unpack(sent[device])[0:tracers]) * flow[here, :],
             block[here, :],
             column[here, :],
             rows,
@@ -413,21 +420,22 @@
 def exchange(tracers, sections, ring, resid, slope, flux, other, block, column, flow, *surface):
     devices, slots = block.shape
     surf_rows = surface[-1].shape[0]
-    landing = pltpu.VMEM((devices, tracers * slots // LANES, LANES), jnp.float32)
+    outgoing = pltpu.VMEM((devices, (tracers + 1) * slots // LANES, LANES), jnp.float32)
+    homecoming = pltpu.VMEM((devices, tracers * slots // LANES, LANES), jnp.float32)
     return pl.pallas_call(
         functools.partial(exchange_kernel, tracers, sections, ring),
         out_shape=[
             jax.ShapeDtypeStruct(resid.shape, jnp.float32),
             jax.ShapeDtypeStruct((tracers * surf_rows, LANES), jnp.float32),
         ],
-        in_specs=[pl.BlockSpec(memory_space=pltpu.VMEM)] * 12,
+        in_specs=[pl.BlockSpec(memory_space=pltpu.VMEM)] * 13,
         out_specs=[pl.BlockSpec(memory_space=pltpu.VMEM)] * 2,
         scratch_shapes=[
-            landing,
-            landing,
-            landing,
-            landing,
-            pltpu.VMEM(((tracers + 1) * surf_rows, LANES), jnp.float32),
+            outgoing,
+            outgoing,
+            homecoming,
+            homecoming,
+            pltpu.VMEM(((tracers + 1) * (-(-surf_rows // 16) * 16), LANES), jnp.float32),
             pltpu.SemaphoreType.DMA((devices,)),
             pltpu.SemaphoreType.DMA((devices,)),
             pltpu.SemaphoreType.DMA((devices,)),
@@ -463,7 +471,8 @@
     cap_rows = -(-capacity // LANES)
     padding = ((0, 0), (0, cap_rows * LANES - capacity))
 
-    handed = lax.ppermute(descend_end(air_state, mix_coef), "sect", [(0, 1)])
+    air = jnp.swapaxes(air_state, 0, 1)
+    handed = lax.ppermute(descend_end(air, mix_coef), "sect", [(0, 1)])
     slots = setup(
         cell_owner.reshape(-1, LANES),
         cell_column.reshape(-1, LANES),
@@ -477,13 +486,12 @@
     slots = slots.reshape(4, devices, cap_rows * LANES)
     block = slots[0].astype(jnp.int32)
     column = slots[1].astype(jnp.int32)
-    gain = lax.all_to_all(slots[2], ("sect", "cols"), split_axis=0, concat_axis=0, tiled=True)
     cell = jnp.pad(slot_cell.reshape(devices, capacity), padding)
-    coupling = gain * jnp.pad(slot_frac.reshape(devices, capacity), padding)
+    frac = jnp.pad(slot_frac.reshape(devices, capacity), padding)
     row, lane = cell // LANES, cell % LANES
 
     last = jnp.where(is_lower, flux_scale, mix_coef[-1])[None]
-    parts, ratios, ends = descend(air_state, mix_coef, handed, last)
+    parts, ratios, ends = descend(air, mix_coef, handed, last)
     received = lax.ppermute(ends, "sect", [(1, 0)])
     low = jnp.where(is_lower, ends, received)
     resid = low[0, :tracers].reshape(tracers * rows, LANES)
@@ -504,7 +512,8 @@
             block,
             column,
             slots[3],
-            coupling,
+            slots[2],
+            frac,
             row,
             lane,
             sea,
@@ -513,7 +522,7 @@
         other = lax.ppermute(flux, "sect", [(0, 1), (1, 0)])
     flux_col = (flux + other).reshape(tracers, columns)
     below = jnp.where(is_lower, flux_col, low[1, :tracers] + low[1, tracers] * flux_col)
-    return (ascend(parts, ratios, below), sea.reshape(tracers, surf_cells))
+    return (jnp.swapaxes(ascend(parts, ratios, below), 0, 1), sea.reshape(tracers, surf_cells))
 
 
 def solution(mesh):

time: 143 us -> 134 us (0.937)
  Pallas kernels: 106 us -> 113 us
  local copies, waits for them, and re-layouts: 19.4 us -> 12.4 us
  starting transfers between devices: 10.8 us -> 3.96 us
    unnamed x30 -> x32, local copies, waits for them, and re-layouts: 18.3 us -> 11.3 us
    all_to_all x1 -> x0, starting transfers between devices: 6.68 us -> none  [body(): lax.all_to_all(slots[2], ('sect', 'cols'), split_axis=0, concat_axis=0, t...]
    pallas_call x2, Pallas kernels: 78.3 us -> 81.2 us  [exchange(): pl.pallas_call(functools.partial(exchange_kernel, tracers, sections, ring...]
    pallas_call x1, Pallas kernels: 1.95 us -> 4.43 us  [ascend(): pl.pallas_call(ascend_kernel, grid=(columns // COL_TILE,), in_specs=[pl.B...]
  transfers between devices with their start and end apart: 5 -> 4, of which waited for: 3 -> 3; matrix products, arithmetic and copies ran while one was open for 1% -> 1% of each run, Pallas kernels for 16% -> 13%
where the time goes in v3:
time: 134 us
  Pallas kernels  113 us (84%)
  local copies, waits for them, and re-layouts  12.4 us (9%)
  starting transfers between devices  3.96 us (3%)
  waiting for transfers between devices  3.91 us (3%)
    pallas_call x2, Pallas kernels, exchange(): pl.pallas_call(functools.partial(exchange_kernel, tracers, sections, ring...  81.2 us
    pallas_call x1, Pallas kernels, setup(): pl.pallas_call(functools.partial(setup_kernel, devices, cap_rows), out_sh...  17.6 us
    unnamed x32, local copies, waits for them, and re-layouts  11.3 us
    pallas_call x1, Pallas kernels, descend(): pl.pallas_call(descend_kernel, grid=(columns // COL_TILE,), in_specs=[pl....  5.2 us
    pallas_call x1, Pallas kernels, ascend(): pl.pallas_call(ascend_kernel, grid=(columns // COL_TILE,), in_specs=[pl.B...  4.43 us
    pallas_call x1, Pallas kernels, descend_end(): pl.pallas_call(descend_end_kernel, grid=(columns // COL_TILE,), in_specs=...  4.15 us
  transfers between devices with their start and end apart: 4, of which 3 were waited for; matrix products, arithmetic and copies ran while one was open for 1% of the time, Pallas kernels for 13%

profile of v3, /device:TPU:0, one launch (start us, length us, event | category | flops | bytes accessed | tf_op | source)
XLA Modules:
  0.0 134.2 jit_solution(15468610577228355649)
XLA Ops:
  0.6 0.0 copy-start.15
  0.6 0.0 copy-start
  0.7 2.3 %copy-done = f32[32,6,6144]{2,0,1:T(8,128)S(1)} copy-done((f32[32,6,6144]{2,0,1:T(8,128)S(1)}, f32[32,6,6144]{2,0,1:T(8,128)}, u32[]{:S(2)}) %copy-start) | copy-done | bytes 4718616
  3.0 0.0 copy-start.4
  3.0 1.1 copy-done.4
  4.1 0.0 copy-start.7
  4.1 0.0 copy-start.8
  4.1 0.0 copy-start.9
  4.1 0.0 copy-start.10
  4.1 0.0 copy-start.14
  4.1 0.0 copy-start.5
  4.2 4.2 %shard_map.131 = f32[7,6144]{1,0:T(8,128)S(1)} custom-call(f32[6,32,6144]{2,1,0:T(8,128)S(1)} %bitcast.18, f32[32,6144]{1,0:T(8,128)S(1)} %copy-done.4), custom_call_target="tpu_custom_call" | custom-call | tf_op jit(solution)/shard_map/pallas_call | solution.py:157
  8.3 0.0 copy-start.12
  8.3 0.0 copy-start.13
  8.3 0.0 copy-start.11
  8.3 2.5 %collective-permute-start = (f32[7,6144]{1,0:T(8,128)S(1)}, f32[7,6144]{1,0:T(8,128)S(1)}, u32[]{:S(2)}, u32[]{:S(2)}) collective-permute-start(f32[7,6144]{1,0:T(8,128)S(1)} %shard_map.131), channel_id=1, source_target_pairs={{0,16},{1,17},{2,18},{3,19},{4,20},{5,21},{6,22},{7,23},{8,24},{9,... | collective-permute-start | bytes 516104 | tf_op jit(solution)/shard_map/ppermute | solution.py:475
  10.9 0.0 copy-done.15
  10.9 0.1 broadcast_in_dim.16.counts
  11.0 0.0 copy-done.7
  11.0 0.0 copy-done.8
  11.0 0.0 copy-done.9
  11.0 0.0 copy-done.10
  11.0 17.6 %shard_map.133 = f32[4,128,128]{2,1,0:T(8,128)S(1)} custom-call(s32[96,128]{1,0:T(8,128)S(1)} %bitcast.25, s32[96,128]{1,0:T(8,128)S(1)} %bitcast.26, f32[96,128]{1,0:T(8,128)S(1)} %bitcast.27, f32[96,128]{1,0:T(8,128)S(1)} %bitcast.28, s32[48,128]{1,0:T(8,128)S(1)} %broadcast_in_dim.16.counts), custom_call_target="tpu_custom_call" | custom-call | tf_op jit(solution)/shard_map/pallas_call | solution.py:127
  28.6 0.0 copy-done.14
  28.6 0.0 collective-permute-done.start
  28.7 0.0 copy-done.5
  28.7 0.0 copy-start.1
  28.7 2.3 %copy-done.1 = f32[32,6,6144]{2,0,1:T(8,128)S(1)} copy-done((f32[32,6,6144]{2,0,1:T(8,128)S(1)}, f32[32,6,6144]{2,0,1:T(8,128)}, u32[]{:S(2)}) %copy-start.1) | copy-done | bytes 4718616
  31.0 0.0 copy-start.6
  31.0 5.2 %shard_map.132 = (f32[32,6,6144]{2,1,0:T(8,128)S(1)}, f32[32,6144]{1,0:T(8,128)S(1)}, f32[2,7,6144]{2,1,0:T(8,128)S(1)}) custom-call(f32[6,32,6144]{2,1,0:T(8,128)S(1)} %bitcast.19, f32[32,6144]{1,0:T(8,128)S(1)} %copy-done.5, f32[7,6144]{1,0:T(8,128)S(1)} %collective-permute-done.start, f32[1,6144]{1,0:T(1,128)S(1)} %bitcast.22), custom_call_target="tpu_custom_call" | custom-call | tf_op jit(solution)/shard_map/pallas_call | solution.py:194
  36.2 0.0 copy-start.2
  36.2 2.6 %copy-done.2 = f32[32,6,6144]{2,1,0:T(8,128)} copy-done((f32[32,6,6144]{2,1,0:T(8,128)}, f32[32,6,6144]{2,1,0:T(8,128)S(1)}, u32[]{:S(2)}) %copy-start.2) | copy-done | bytes 4718616
  38.9 1.3 collective-permute-start.1
  40.3 0.0 copy-done.12
  40.3 0.1 reshape.52
  40.4 0.0 copy-done.13
  40.4 0.1 reshape.51
  40.5 0.0 copy-done.11
  40.5 0.1 add_select_fusion
  40.6 1.9 %collective-permute-done.1 = f32[2,7,6144]{2,1,0:T(8,128)S(1)} collective-permute-done((f32[2,7,6144]{2,1,0:T(8,128)S(1)}, f32[2,7,6144]{2,1,0:T(8,128)S(1)}, u32[]{:S(2)}, u32[]{:S(2)}) %collective-permute-start.1) | collective-permute-done | bytes 344096 | tf_op jit(solution)/shard_map/ppermute | solution.py:495
  42.5 0.1 broadcast_select_fusion
  42.6 0.1 fusion.4
  42.7 0.0 copy-done.6
  42.7 43.5 %shard_map.134 = (f32[288,128]{1,0:T(8,128)S(1)}, f32[144,128]{1,0:T(8,128)S(1)}) custom-call(f32[288,128]{1,0:T(8,128)S(1)} %reshape_squeeze.6.resid, f32[48,128]{1,0:T(8,128)S(1)} %bitcast.20, f32[288,128]{1,0:T(8,128)S(1)} %broadcast_in_dim.14.flux.other, f32[288,128]{1,0:T(8,128)S(1)} %broadcast_in_dim.14.flux.other, ...), custom_call_target="tpu_custom_call" | custom-call | tf_op jit(solution)/shard_map/pallas_call | solution.py:425
  86.2 0.1 collective-permute-start.2
  86.3 1.4 %collective-permute-done.2.other = f32[288,128]{1,0:T(8,128)S(1)} collective-permute-done((f32[288,128]{1,0:T(8,128)S(1)}, f32[288,128]{1,0:T(8,128)S(1)}, u32[]{:S(2)}, u32[]{:S(2)}) %collective-permute-start.2) | collective-permute-done | bytes 147488 | tf_op jit(solution)/shard_map/ppermute | solution.py:522
  87.7 37.8 %shard_map.135 = (f32[288,128]{1,0:T(8,128)S(1)}, f32[144,128]{1,0:T(8,128)S(1)}) custom-call(f32[288,128]{1,0:T(8,128)S(1)} %reshape_squeeze.6.resid, f32[48,128]{1,0:T(8,128)S(1)} %bitcast.21, f32[288,128]{1,0:T(8,128)S(1)} %get-tuple-element.12.flux, f32[288,128]{1,0:T(8,128)S(1)} %collective-permute-done.2.other, ...), custom_call_target="tpu_custom_call" | custom-call | tf_op jit(solution)/shard_map/pallas_call | solution.py:425
  125.4 0.1 collective-permute-start.3
  125.5 0.7 reshape.56
  126.2 0.7 collective-permute-done.3
  127.0 0.0 copy-start.3
  127.0 2.8 %copy-done.3 = f32[32,6,6144]{2,1,0:T(8,128)S(1)} copy-done((f32[32,6,6144]{2,1,0:T(8,128)S(1)}, f32[32,6,6144]{2,1,0:T(8,128)}, u32[]{:S(2)}) %copy-start.3) | copy-done | bytes 4718616
  129.8 4.4 %shard_map.136 = f32[6,32,6144]{2,1,0:T(8,128)} custom-call(f32[32,6,6144]{2,1,0:T(8,128)S(1)} %copy-done.3, f32[32,6144]{1,0:T(8,128)S(1)} %get-tuple-element.10.ratios, f32[6,6144]{1,0:T(8,128)S(1)} %fusion.1.below), custom_call_target="tpu_custom_call" | custom-call | tf_op jit(solution)/shard_map/pallas_call | solution.py:228
  (15 shorter events, 0.3 us)
Async XLA Ops:
  0.6 10.3 %copy-start.15 = (s32[1,48]{1,0:T(1,128)S(1)}, s32[1,48]{1,0:T(1,128)}, u32[]{:S(2)}) copy-start(s32[1,48]{1,0:T(1,128)} %param.17) | copy-start | bytes 580
  0.6 2.3 %copy-start = (f32[32,6,6144]{2,0,1:T(8,128)S(1)}, f32[32,6,6144]{2,0,1:T(8,128)}, u32[]{:S(2)}) copy-start(f32[32,6,6144]{2,0,1:T(8,128)} %param.12) | copy-start | bytes 14155780
  3.0 1.1 copy-start.4
  4.1 6.9 %copy-start.7 = (s32[12288,1]{0,1:T(1,128)S(1)}, s32[12288,1]{0,1:T(1,128)}, u32[]{:S(2)}) copy-start(s32[12288,1]{0,1:T(1,128)} %param.19) | copy-start | bytes 147460
  4.1 6.9 %copy-start.8 = (s32[12288]{0:T(1024)S(1)}, s32[12288]{0:T(1024)}, u32[]{:S(2)}) copy-start(s32[12288]{0:T(1024)} %param.18) | copy-start | bytes 147460
  4.1 6.9 %copy-start.9 = (f32[12288]{0:T(1024)S(1)}, f32[12288]{0:T(1024)}, u32[]{:S(2)}) copy-start(f32[12288]{0:T(1024)} %param.20) | copy-start | bytes 147460
  4.1 6.9 %copy-start.10 = (f32[12288]{0:T(1024)S(1)}, f32[12288]{0:T(1024)}, u32[]{:S(2)}) copy-start(f32[12288]{0:T(1024)} %param.21) | copy-start | bytes 147460
  4.1 24.5 %copy-start.14 = (f32[6144]{0:T(1024)S(1)}, f32[6144]{0:T(1024)}, u32[]{:S(2)}) copy-start(f32[6144]{0:T(1024)} %param.14) | copy-start | bytes 73732
  4.1 24.5 %copy-start.5 = (f32[32,6144]{1,0:T(8,128)S(1)}, f32[32,6144]{1,0:T(8,128)}, u32[]{:S(2)}) copy-start(f32[32,6144]{1,0:T(8,128)} %mix.3) | copy-start | bytes 2359300
  8.3 32.0 %copy-start.12 = (s32[15360]{0:T(1024)S(1)}, s32[15360]{0:T(1024)}, u32[]{:S(2)}) copy-start(s32[15360]{0:T(1024)} %param.22) | copy-start | bytes 184324
  8.3 32.1 %copy-start.13 = (f32[15360]{0:T(1024)S(1)}, f32[15360]{0:T(1024)}, u32[]{:S(2)}) copy-start(f32[15360]{0:T(1024)} %param.23) | copy-start | bytes 184324
  8.3 32.2 %copy-start.11 = (f32[6,3072]{1,0:T(8,128)S(1)}, f32[6,3072]{1,0:T(8,128)}, u32[]{:S(2)}) copy-start(f32[6,3072]{1,0:T(8,128)} %param.15) | copy-start | bytes 221188
  8.3 20.3 %collective-permute-start = (f32[7,6144]{1,0:T(8,128)S(1)}, f32[7,6144]{1,0:T(8,128)S(1)}, u32[]{:S(2)}, u32[]{:S(2)}) collective-permute-start(f32[7,6144]{1,0:T(8,128)S(1)} %shard_map.131), channel_id=1, source_target_pairs={{0,16},{1,17},{2,18},{3,19},{4,20},{5,21},{6,22},{7,23},{8,24},{9,... | collective-permute-start | bytes 516104 | tf_op jit(solution)/shard_map/ppermute | solution.py:475
  28.7 2.3 %copy-start.1 = (f32[32,6,6144]{2,0,1:T(8,128)S(1)}, f32[32,6,6144]{2,0,1:T(8,128)}, u32[]{:S(2)}) copy-start(f32[32,6,6144]{2,0,1:T(8,128)} %param.12) | copy-start | bytes 14155780
  31.0 11.7 %copy-start.6 = (f32[3072]{0:T(1024)S(1)}, f32[3072]{0:T(1024)}, u32[]{:S(2)}) copy-start(f32[3072]{0:T(1024)} %param.16) | copy-start | bytes 36868
  36.2 2.7 %copy-start.2 = (f32[32,6,6144]{2,1,0:T(8,128)}, f32[32,6,6144]{2,1,0:T(8,128)S(1)}, u32[]{:S(2)}) copy-start(f32[32,6,6144]{2,1,0:T(8,128)S(1)} %get-tuple-element.9.parts) | copy-start | bytes 14155780
  38.9 3.6 %collective-permute-start.1 = (f32[2,7,6144]{2,1,0:T(8,128)S(1)}, f32[2,7,6144]{2,1,0:T(8,128)S(1)}, u32[]{:S(2)}, u32[]{:S(2)}) collective-permute-start(f32[2,7,6144]{2,1,0:T(8,128)S(1)} %get-tuple-element.11), channel_id=1, source_target_pairs={{16,0},{17,1},{18,2},{19,3},{20,4},{21,5},{22,6},{23,7},{24,8},{25... | collective-permute-start | bytes 1032200 | tf_op jit(solution)/shard_map/ppermute | solution.py:495
  86.2 1.4 %collective-permute-start.2 = (f32[288,128]{1,0:T(8,128)S(1)}, f32[288,128]{1,0:T(8,128)S(1)}, u32[]{:S(2)}, u32[]{:S(2)}) collective-permute-start(f32[288,128]{1,0:T(8,128)S(1)} %get-tuple-element.12.flux), channel_id=1, source_target_pairs={{0,16},{16,0},{1,17},{17,1},{2,18},{18,2},{3,19},{19,3},{4,20},{20... | collective-permute-start | bytes 442376 | tf_op jit(solution)/shard_map/ppermute | solution.py:522
  125.4 1.4 %collective-permute-start.3 = (f32[288,128]{1,0:T(8,128)S(1)}, f32[288,128]{1,0:T(8,128)S(1)}, u32[]{:S(2)}, u32[]{:S(2)}) collective-permute-start(f32[288,128]{1,0:T(8,128)S(1)} %get-tuple-element.14), channel_id=1, source_target_pairs={{0,16},{16,0},{1,17},{17,1},{2,18},{18,2},{3,19},{19,3},{4,20},{20... | collective-permute-start | bytes 442376 | tf_op jit(solution)/shard_map/ppermute | solution.py:522
  127.0 2.8 %copy-start.3 = (f32[32,6,6144]{2,1,0:T(8,128)S(1)}, f32[32,6,6144]{2,1,0:T(8,128)}, u32[]{:S(2)}) copy-start(f32[32,6,6144]{2,1,0:T(8,128)} %copy-done.2) | copy-start | bytes 14155780

commit v4 on v3

--- a/solution.py
+++ b/solution.py
@@ -314,6 +314,18 @@
         count = values.shape[0] // parts
         return jnp.concatenate([values[p * count : (p + 1) * count] for p in range(parts)], axis=1)
 
+    def rows_of(ref, sources):
+        return jnp.concatenate([ref[pl.ds(source, 1), :] for source in sources], axis=1)
+
+    def in_pairs(act):
+        act(1)
+
+        def both(p, _):
+            act(2 * p, 2 * p + 1)
+            return 0
+
+        lax.fori_loop(1, devices // 2, both, 0)
+
     barrier = pltpu.get_barrier_semaphore()
 
     def greet(s, _):
@@ -338,36 +350,35 @@
     sent[me] = own
     pl.semaphore_wait(barrier, devices - 1)
 
-    def send(s, _):
-        device = ahead(s)
-        sent[device] = at_cells(device)
-        outward(s).start()
-        return 0
-
-    lax.fori_loop(1, devices, send, 0)
+    def send(*steps):
+        chunks = [at_cells(ahead(s)) for s in steps]
+        for s, chunk in zip(steps, chunks):
+            sent[ahead(s)] = chunk
+        for s in steps:
+            outward(s).start()
+
+    in_pairs(send)
     acc[...] = jnp.zeros_like(acc)
 
-    def add(values, device):
-        here = pl.ds(device, 1)
-        came = unpack(values)
-        strength = came[tracers:] * frac[here, :]
+    def add(chunks, sources):
+        came = jnp.concatenate([unpack(chunk) for chunk in chunks], axis=1)
+        strength = came[tracers:] * rows_of(frac, sources)
         scatter_step(
             acc,
             jnp.concatenate([came[0:tracers] * strength, strength], axis=0),
-            row[here, :],
-            lane[here, :],
+            rows_of(row, sources),
+            rows_of(lane, sources),
             acc_rows,
         )
 
-    add(own, me)
-
-    def receive(s, _):
-        outward(s).wait_recv()
-        device = behind(s)
-        add(arrived[device], device)
-        return 0
-
-    lax.fori_loop(1, devices, receive, 0)
+    add([own], [me])
+
+    def receive(*steps):
+        for s in steps:
+            outward(s).wait_recv()
+        add([arrived[behind(s)] for s in steps], [behind(s) for s in steps])
+
+    in_pairs(receive)
     pace = rate[...]
     inverse = 1.0 / (1.0 + pace * acc[tracers * acc_rows : tracers * acc_rows + surf_rows])
     for q in range(tracers):
@@ -380,34 +391,37 @@
         here = pl.ds(device, 1)
         return pack(gather_step(sea_table, row[here, :], lane[here, :], surf_rows, tracers))
 
-    def give_back(s, _):
-        device = ahead(s)
-        back[device] = seen(device)
-        homeward(s).start()
-        return 0
-
-    lax.fori_loop(1, devices, give_back, 0)
+    def give_back(*steps):
+        chunks = [seen(ahead(s)) for s in steps]
+        for s, chunk in zip(steps, chunks):
+            back[ahead(s)] = chunk
+        for s in steps:
+            homeward(s).start()
+
+    in_pairs(give_back)
     flux_new[...] = jnp.zeros_like(flux_new)
 
-    def collect(values, device):
-        here = pl.ds(device, 1)
+    def collect(chunks, sources):
+        change = [
+            unpack(chunk) - unpack(sent[source])[0:tracers]
+            for chunk, source in zip(chunks, sources)
+        ]
         scatter_step(
             flux_new,
-            (unpack(values) - unpack(sent[device])[0:tracers]) * flow[here, :],
-            block[here, :],
-            column[here, :],
+            jnp.concatenate(change, axis=1) * rows_of(flow, sources),
+            rows_of(block, sources),
+            rows_of(column, sources),
             rows,
         )
 
-    collect(seen(me), me)
-
-    def take_back(s, _):
-        homeward(s).wait_recv()
-        device = behind(s)
-        collect(returned[device], device)
-        return 0
-
-    lax.fori_loop(1, devices, take_back, 0)
+    collect([seen(me)], [me])
+
+    def take_back(*steps):
+        for s in steps:
+            homeward(s).wait_recv()
+        collect([returned[behind(s)] for s in steps], [behind(s) for s in steps])
+
+    in_pairs(take_back)
 
     def finish(s, _):
         outward(s).wait_send()

time: 134 us -> 124 us (0.925)
  Pallas kernels: 113 us -> 102 us
    pallas_call x2, Pallas kernels: 81.2 us -> 70.8 us  [exchange(): pl.pallas_call(functools.partial(exchange_kernel, tracers, sections, ring...]
  transfers between devices with their start and end apart: 4 -> 4, of which waited for: 3 -> 3; matrix products, arithmetic and copies ran while one was open for 1% -> 1% of each run, Pallas kernels for 13% -> 14%
where the time goes in v4:
time: 124 us
  Pallas kernels  102 us (82%)
  local copies, waits for them, and re-layouts  12.4 us (10%)
  waiting for transfers between devices  3.95 us (3%)
  starting transfers between devices  3.92 us (3%)
    pallas_call x2, Pallas kernels, exchange(): pl.pallas_call(functools.partial(exchange_kernel, tracers, sections, ring...  70.8 us
    pallas_call x1, Pallas kernels, setup(): pl.pallas_call(functools.partial(setup_kernel, devices, cap_rows), out_sh...  17.6 us
    unnamed x32, local copies, waits for them, and re-layouts  11.3 us
    pallas_call x1, Pallas kernels, descend(): pl.pallas_call(descend_kernel, grid=(columns // COL_TILE,), in_specs=[pl....  5.2 us
    pallas_call x1, Pallas kernels, ascend(): pl.pallas_call(ascend_kernel, grid=(columns // COL_TILE,), in_specs=[pl.B...  4.43 us
    pallas_call x1, Pallas kernels, descend_end(): pl.pallas_call(descend_end_kernel, grid=(columns // COL_TILE,), in_specs=...  4.15 us
    ppermute x1, starting transfers between devices, body(): handed = lax.ppermute(descend_end(air, mix_coef), 'sect', [(0, 1)])  2.5 us
  transfers between devices with their start and end apart: 4, of which 3 were waited for; matrix products, arithmetic and copies ran while one was open for 1% of the time, Pallas kernels for 14%

profile of v4, /device:TPU:0, one launch (start us, length us, event | category | flops | bytes accessed | tf_op | source)
XLA Modules:
  0.0 123.8 jit_solution(1873392087656431110)
XLA Ops:
  0.6 0.0 copy-start.15
  0.6 0.0 copy-start
  0.7 2.3 %copy-done = f32[32,6,6144]{2,0,1:T(8,128)S(1)} copy-done((f32[32,6,6144]{2,0,1:T(8,128)S(1)}, f32[32,6,6144]{2,0,1:T(8,128)}, u32[]{:S(2)}) %copy-start) | copy-done | bytes 4718616
  3.0 0.0 copy-start.4
  3.0 1.1 copy-done.4
  4.1 0.0 copy-start.7
  4.1 0.0 copy-start.8
  4.1 0.0 copy-start.9
  4.1 0.0 copy-start.10
  4.1 0.0 copy-start.14
  4.1 0.0 copy-start.5
  4.2 4.2 %shard_map.131 = f32[7,6144]{1,0:T(8,128)S(1)} custom-call(f32[6,32,6144]{2,1,0:T(8,128)S(1)} %bitcast.18, f32[32,6144]{1,0:T(8,128)S(1)} %copy-done.4), custom_call_target="tpu_custom_call" | custom-call | tf_op jit(solution)/shard_map/pallas_call | solution.py:157
  8.3 0.0 copy-start.12
  8.3 0.0 copy-start.13
  8.3 0.0 copy-start.11
  8.3 2.5 %collective-permute-start = (f32[7,6144]{1,0:T(8,128)S(1)}, f32[7,6144]{1,0:T(8,128)S(1)}, u32[]{:S(2)}, u32[]{:S(2)}) collective-permute-start(f32[7,6144]{1,0:T(8,128)S(1)} %shard_map.131), channel_id=1, source_target_pairs={{0,16},{1,17},{2,18},{3,19},{4,20},{5,21},{6,22},{7,23},{8,24},{9,... | collective-permute-start | bytes 516104 | tf_op jit(solution)/shard_map/ppermute | solution.py:489
  10.9 0.0 copy-done.15
  10.9 0.1 broadcast_in_dim.16.counts
  11.0 0.0 copy-done.7
  11.0 0.0 copy-done.8
  11.0 0.0 copy-done.9
  11.0 0.0 copy-done.10
  11.0 17.6 %shard_map.133 = f32[4,128,128]{2,1,0:T(8,128)S(1)} custom-call(s32[96,128]{1,0:T(8,128)S(1)} %bitcast.25, s32[96,128]{1,0:T(8,128)S(1)} %bitcast.26, f32[96,128]{1,0:T(8,128)S(1)} %bitcast.27, f32[96,128]{1,0:T(8,128)S(1)} %bitcast.28, s32[48,128]{1,0:T(8,128)S(1)} %broadcast_in_dim.16.counts), custom_call_target="tpu_custom_call" | custom-call | tf_op jit(solution)/shard_map/pallas_call | solution.py:127
  28.6 0.0 copy-done.14
  28.6 0.0 collective-permute-done.start
  28.7 0.0 copy-done.5
  28.7 0.0 copy-start.1
  28.7 2.3 %copy-done.1 = f32[32,6,6144]{2,0,1:T(8,128)S(1)} copy-done((f32[32,6,6144]{2,0,1:T(8,128)S(1)}, f32[32,6,6144]{2,0,1:T(8,128)}, u32[]{:S(2)}) %copy-start.1) | copy-done | bytes 4718616
  31.0 0.0 copy-start.6
  31.0 5.2 %shard_map.132 = (f32[32,6,6144]{2,1,0:T(8,128)S(1)}, f32[32,6144]{1,0:T(8,128)S(1)}, f32[2,7,6144]{2,1,0:T(8,128)S(1)}) custom-call(f32[6,32,6144]{2,1,0:T(8,128)S(1)} %bitcast.19, f32[32,6144]{1,0:T(8,128)S(1)} %copy-done.5, f32[7,6144]{1,0:T(8,128)S(1)} %collective-permute-done.start, f32[1,6144]{1,0:T(1,128)S(1)} %bitcast.22), custom_call_target="tpu_custom_call" | custom-call | tf_op jit(solution)/shard_map/pallas_call | solution.py:194
  36.2 0.0 copy-start.2
  36.2 2.6 %copy-done.2 = f32[32,6,6144]{2,1,0:T(8,128)} copy-done((f32[32,6,6144]{2,1,0:T(8,128)}, f32[32,6,6144]{2,1,0:T(8,128)S(1)}, u32[]{:S(2)}) %copy-start.2) | copy-done | bytes 4718616
  38.9 1.3 %collective-permute-start.1 = (f32[2,7,6144]{2,1,0:T(8,128)S(1)}, f32[2,7,6144]{2,1,0:T(8,128)S(1)}, u32[]{:S(2)}, u32[]{:S(2)}) collective-permute-start(f32[2,7,6144]{2,1,0:T(8,128)S(1)} %get-tuple-element.11), channel_id=1, source_target_pairs={{16,0},{17,1},{18,2},{19,3},{20,4},{21,5},{22,6},{23,7},{24,8},{25... | collective-permute-start | bytes 1032200 | tf_op jit(solution)/shard_map/ppermute | solution.py:509
  40.3 0.0 copy-done.12
  40.3 0.1 reshape.52
  40.4 0.0 copy-done.13
  40.4 0.1 reshape.51
  40.5 0.0 copy-done.11
  40.5 0.1 add_select_fusion
  40.6 1.9 %collective-permute-done.1 = f32[2,7,6144]{2,1,0:T(8,128)S(1)} collective-permute-done((f32[2,7,6144]{2,1,0:T(8,128)S(1)}, f32[2,7,6144]{2,1,0:T(8,128)S(1)}, u32[]{:S(2)}, u32[]{:S(2)}) %collective-permute-start.1) | collective-permute-done | bytes 344096 | tf_op jit(solution)/shard_map/ppermute | solution.py:509
  42.5 0.1 broadcast_select_fusion
  42.6 0.1 fusion.4
  42.7 0.0 copy-done.6
  42.7 36.2 %shard_map.134 = (f32[288,128]{1,0:T(8,128)S(1)}, f32[144,128]{1,0:T(8,128)S(1)}) custom-call(f32[288,128]{1,0:T(8,128)S(1)} %reshape_squeeze.6.resid, f32[48,128]{1,0:T(8,128)S(1)} %bitcast.20, f32[288,128]{1,0:T(8,128)S(1)} %broadcast_in_dim.14.flux.other, f32[288,128]{1,0:T(8,128)S(1)} %broadcast_in_dim.14.flux.other, ...), custom_call_target="tpu_custom_call" | custom-call | tf_op jit(solution)/shard_map/pallas_call | solution.py:439
  78.9 0.1 collective-permute-start.2
  79.0 1.4 %collective-permute-done.2.other = f32[288,128]{1,0:T(8,128)S(1)} collective-permute-done((f32[288,128]{1,0:T(8,128)S(1)}, f32[288,128]{1,0:T(8,128)S(1)}, u32[]{:S(2)}, u32[]{:S(2)}) %collective-permute-start.2) | collective-permute-done | bytes 147488 | tf_op jit(solution)/shard_map/ppermute | solution.py:536
  80.3 34.7 %shard_map.135 = (f32[288,128]{1,0:T(8,128)S(1)}, f32[144,128]{1,0:T(8,128)S(1)}) custom-call(f32[288,128]{1,0:T(8,128)S(1)} %reshape_squeeze.6.resid, f32[48,128]{1,0:T(8,128)S(1)} %bitcast.21, f32[288,128]{1,0:T(8,128)S(1)} %get-tuple-element.12.flux, f32[288,128]{1,0:T(8,128)S(1)} %collective-permute-done.2.other, ...), custom_call_target="tpu_custom_call" | custom-call | tf_op jit(solution)/shard_map/pallas_call | solution.py:439
  115.0 0.1 collective-permute-start.3
  115.1 0.7 reshape.56
  115.8 0.7 collective-permute-done.3
  116.6 0.0 copy-start.3
  116.6 2.8 %copy-done.3 = f32[32,6,6144]{2,1,0:T(8,128)S(1)} copy-done((f32[32,6,6144]{2,1,0:T(8,128)S(1)}, f32[32,6,6144]{2,1,0:T(8,128)}, u32[]{:S(2)}) %copy-start.3) | copy-done | bytes 4718616
  119.4 4.4 %shard_map.136 = f32[6,32,6144]{2,1,0:T(8,128)} custom-call(f32[32,6,6144]{2,1,0:T(8,128)S(1)} %copy-done.3, f32[32,6144]{1,0:T(8,128)S(1)} %get-tuple-element.10.ratios, f32[6,6144]{1,0:T(8,128)S(1)} %fusion.1.below), custom_call_target="tpu_custom_call" | custom-call | tf_op jit(solution)/shard_map/pallas_call | solution.py:228
  (15 shorter events, 0.3 us)
Async XLA Ops:
  0.6 10.3 %copy-start.15 = (s32[1,48]{1,0:T(1,128)S(1)}, s32[1,48]{1,0:T(1,128)}, u32[]{:S(2)}) copy-start(s32[1,48]{1,0:T(1,128)} %param.17) | copy-start | bytes 580
  0.6 2.3 %copy-start = (f32[32,6,6144]{2,0,1:T(8,128)S(1)}, f32[32,6,6144]{2,0,1:T(8,128)}, u32[]{:S(2)}) copy-start(f32[32,6,6144]{2,0,1:T(8,128)} %param.12) | copy-start | bytes 14155780
  3.0 1.1 copy-start.4
  4.1 6.9 %copy-start.7 = (s32[12288,1]{0,1:T(1,128)S(1)}, s32[12288,1]{0,1:T(1,128)}, u32[]{:S(2)}) copy-start(s32[12288,1]{0,1:T(1,128)} %param.19) | copy-start | bytes 147460
  4.1 6.9 %copy-start.8 = (s32[12288]{0:T(1024)S(1)}, s32[12288]{0:T(1024)}, u32[]{:S(2)}) copy-start(s32[12288]{0:T(1024)} %param.18) | copy-start | bytes 147460
  4.1 6.9 %copy-start.9 = (f32[12288]{0:T(1024)S(1)}, f32[12288]{0:T(1024)}, u32[]{:S(2)}) copy-start(f32[12288]{0:T(1024)} %param.20) | copy-start | bytes 147460
  4.1 6.9 %copy-start.10 = (f32[12288]{0:T(1024)S(1)}, f32[12288]{0:T(1024)}, u32[]{:S(2)}) copy-start(f32[12288]{0:T(1024)} %param.21) | copy-start | bytes 147460
  4.1 24.5 %copy-start.14 = (f32[6144]{0:T(1024)S(1)}, f32[6144]{0:T(1024)}, u32[]{:S(2)}) copy-start(f32[6144]{0:T(1024)} %param.14) | copy-start | bytes 73732
  4.1 24.5 %copy-start.5 = (f32[32,6144]{1,0:T(8,128)S(1)}, f32[32,6144]{1,0:T(8,128)}, u32[]{:S(2)}) copy-start(f32[32,6144]{1,0:T(8,128)} %mix.3) | copy-start | bytes 2359300
  8.3 32.0 %copy-start.12 = (s32[15360]{0:T(1024)S(1)}, s32[15360]{0:T(1024)}, u32[]{:S(2)}) copy-start(s32[15360]{0:T(1024)} %param.22) | copy-start | bytes 184324
  8.3 32.1 %copy-start.13 = (f32[15360]{0:T(1024)S(1)}, f32[15360]{0:T(1024)}, u32[]{:S(2)}) copy-start(f32[15360]{0:T(1024)} %param.23) | copy-start | bytes 184324
  8.3 32.2 %copy-start.11 = (f32[6,3072]{1,0:T(8,128)S(1)}, f32[6,3072]{1,0:T(8,128)}, u32[]{:S(2)}) copy-start(f32[6,3072]{1,0:T(8,128)} %param.15) | copy-start | bytes 221188
  8.3 20.3 %collective-permute-start = (f32[7,6144]{1,0:T(8,128)S(1)}, f32[7,6144]{1,0:T(8,128)S(1)}, u32[]{:S(2)}, u32[]{:S(2)}) collective-permute-start(f32[7,6144]{1,0:T(8,128)S(1)} %shard_map.131), channel_id=1, source_target_pairs={{0,16},{1,17},{2,18},{3,19},{4,20},{5,21},{6,22},{7,23},{8,24},{9,... | collective-permute-start | bytes 516104 | tf_op jit(solution)/shard_map/ppermute | solution.py:489
  28.7 2.3 %copy-start.1 = (f32[32,6,6144]{2,0,1:T(8,128)S(1)}, f32[32,6,6144]{2,0,1:T(8,128)}, u32[]{:S(2)}) copy-start(f32[32,6,6144]{2,0,1:T(8,128)} %param.12) | copy-start | bytes 14155780
  31.0 11.7 %copy-start.6 = (f32[3072]{0:T(1024)S(1)}, f32[3072]{0:T(1024)}, u32[]{:S(2)}) copy-start(f32[3072]{0:T(1024)} %param.16) | copy-start | bytes 36868
  36.2 2.7 %copy-start.2 = (f32[32,6,6144]{2,1,0:T(8,128)}, f32[32,6,6144]{2,1,0:T(8,128)S(1)}, u32[]{:S(2)}) copy-start(f32[32,6,6144]{2,1,0:T(8,128)S(1)} %get-tuple-element.9.parts) | copy-start | bytes 14155780
  38.9 3.6 %collective-permute-start.1 = (f32[2,7,6144]{2,1,0:T(8,128)S(1)}, f32[2,7,6144]{2,1,0:T(8,128)S(1)}, u32[]{:S(2)}, u32[]{:S(2)}) collective-permute-start(f32[2,7,6144]{2,1,0:T(8,128)S(1)} %get-tuple-element.11), channel_id=1, source_target_pairs={{16,0},{17,1},{18,2},{19,3},{20,4},{21,5},{22,6},{23,7},{24,8},{25... | collective-permute-start | bytes 1032200 | tf_op jit(solution)/shard_map/ppermute | solution.py:509
  78.9 1.4 %collective-permute-start.2 = (f32[288,128]{1,0:T(8,128)S(1)}, f32[288,128]{1,0:T(8,128)S(1)}, u32[]{:S(2)}, u32[]{:S(2)}) collective-permute-start(f32[288,128]{1,0:T(8,128)S(1)} %get-tuple-element.12.flux), channel_id=1, source_target_pairs={{0,16},{16,0},{1,17},{17,1},{2,18},{18,2},{3,19},{19,3},{4,20},{20... | collective-permute-start | bytes 442376 | tf_op jit(solution)/shard_map/ppermute | solution.py:536
  115.0 1.4 %collective-permute-start.3 = (f32[288,128]{1,0:T(8,128)S(1)}, f32[288,128]{1,0:T(8,128)S(1)}, u32[]{:S(2)}, u32[]{:S(2)}) collective-permute-start(f32[288,128]{1,0:T(8,128)S(1)} %get-tuple-element.14), channel_id=1, source_target_pairs={{0,16},{16,0},{1,17},{17,1},{2,18},{18,2},{3,19},{19,3},{4,20},{20... | collective-permute-start | bytes 442376 | tf_op jit(solution)/shard_map/ppermute | solution.py:536
  116.6 2.8 %copy-start.3 = (f32[32,6,6144]{2,1,0:T(8,128)S(1)}, f32[32,6,6144]{2,1,0:T(8,128)}, u32[]{:S(2)}) copy-start(f32[32,6,6144]{2,1,0:T(8,128)} %copy-done.2) | copy-start | bytes 14155780
